TPU v7x, 256 devices: a whole 4x4x8 slice. The times are simulated.
256 devices in a mesh: blk: 64 (over z, y, x_lo), rep: 4 (over x_hi, core).
Axes of the slice: x: 4 (x_hi: 2, x_lo: 2; x = x_hi * 2 + x_lo), y: 4, z: 8, core: 2. Of those that a mesh axis runs over, the one named last changes fastest.
Arguments:
- embeddings: bfloat16 [65536, 400], P('blk'), may hold values from -1.5 to 1.5
- relations: bfloat16 [2, 400, 400], replicated, may hold values from -0.3125 to 0.3125
- source_index: int32 [2, 256000], P(None, ('blk', 'rep')), may hold values from 0 to 1023
- target_index: int32 [2, 256000], P(None, ('blk', 'rep')), may hold values from 0 to 1023
- negative_index: int32 [2, 512, 1000], P(None, ('blk', 'rep')), may hold values from 0 to 1023
- span_relation: int32 [2, 512], P(None, ('blk', 'rep')), may hold values from 0 to 1
- edge_count: int32 [2, 256], P(None, ('blk', 'rep')), may hold values from 0 to 1000, as said below
Outputs:
- entity_grad: float32 [65536, 400], P(('blk', 'rep'))
- relation_grad: float32 [2, 400, 400], replicated
Inputs may be any that keep to these rules, and one draw needn't show every extreme that they name: For each step and each group of 4 consecutive devices u (those with one blk index), the numbers of spans with a live edge, ceil(edge_count / 500) summed over the group, equal 4; in each such group one device has all 1000 edge slots live.
All inputs are finite; a program needn't handle non-finite values.
Results may differ from a plain program's by a relative error of at most 0.003.
Values may be sent and summed in bfloat16 or wider, within the bound.
A program may use at most 64 MiB of HBM per device.

v0:
```python
import jax
import jax.numpy as jnp
from jax import lax
from jax.sharding import PartitionSpec as P


def from_behind(block, axis, distance):
    devices = range(lax.axis_size(axis))
    route = [((i - distance) % len(devices), i) for i in devices]
    return lax.ppermute(block, axis, route)


def account(embeddings, slab, relations, carry, item):
    source_sum, target_sum, operator_sum = carry
    source_rows, target_rows, negative_rows, relation_id, live_count = item
    width = source_rows.shape[0]
    operator = relations[relation_id]
    source_vectors = embeddings[source_rows]
    target_vectors = slab[target_rows]
    negative_vectors = slab[negative_rows]
    live = (jnp.arange(width) < live_count).astype(jnp.float32)
    query = jnp.dot(source_vectors, operator, preferred_element_type=jnp.float32).astype(
        jnp.bfloat16
    )
    query_wide = query.astype(jnp.float32)
    positive = jnp.sum(query_wide * target_vectors.astype(jnp.float32), axis=1)
    negative = lax.dot_general(
        query, negative_vectors, (((1,), (1,)), ((), ())), preferred_element_type=jnp.float32
    )
    positive_grad = -live * jax.nn.sigmoid(-positive)
    weight = live * negative_vectors.shape[0] ** (-0.5)
    negative_grad = (jax.nn.sigmoid(negative) * weight[:, None]).astype(jnp.bfloat16)
    query_grad = (
        positive_grad[:, None] * target_vectors.astype(jnp.float32)
        + jnp.dot(negative_grad, negative_vectors, preferred_element_type=jnp.float32)
    ).astype(jnp.bfloat16)
    source_grad = lax.dot_general(
        query_grad, operator, (((1,), (1,)), ((), ())), preferred_element_type=jnp.float32
    )
    negative_rows_grad = lax.dot_general(
        negative_grad, query, (((0,), (0,)), ((), ())), preferred_element_type=jnp.float32
    )
    operator_grad = lax.dot_general(
        source_vectors, query_grad, (((0,), (0,)), ((), ())), preferred_element_type=jnp.float32
    )
    selector = (jnp.arange(relations.shape[0]) == relation_id).astype(jnp.float32)
    source_sum = source_sum.at[source_rows].add(source_grad)
    target_sum = target_sum.at[target_rows].add(positive_grad[:, None] * query_wide)
    target_sum = target_sum.at[negative_rows].add(negative_rows_grad)
    operator_sum = operator_sum + selector[:, None, None] * operator_grad
    return ((source_sum, target_sum, operator_sum), None)


def own_lists(source_index, target_index, negative_index, span_relation, edge_count, step):
    slots = span_relation.shape[1]
    source_rows = source_index[step].reshape(slots, -1)
    target_rows = target_index[step].reshape(slots, -1)
    width = source_rows.shape[1]
    live_count = jnp.clip(edge_count[step, 0] - jnp.arange(slots) * width, 0, width)
    return (source_rows, target_rows, negative_index[step], span_relation[step], live_count)


def on_device(
    embeddings, relations, source_index, target_index, negative_index, span_relation, edge_count
):
    steps = source_index.shape[0]
    rows = embeddings.shape[0]
    groups = lax.axis_size("rep")
    share = rows // groups
    slab = embeddings
    source_sum = jnp.zeros(embeddings.shape, jnp.float32)
    returned = jnp.zeros((share, embeddings.shape[1]), jnp.float32)
    operator_total = jnp.zeros(relations.shape, jnp.float32)
    for step in range(steps):
        slab = from_behind(slab, "blk", 1)
        lists = own_lists(
            source_index, target_index, negative_index, span_relation, edge_count, step
        )

        def visit(carry, item):
            return account(embeddings, slab, relations, carry, item)

        start_state = (
            source_sum,
            jnp.zeros(embeddings.shape, jnp.float32),
            jnp.zeros(relations.shape, jnp.float32),
        )
        (source_sum, target_sum, operator_sum), unused = lax.scan(visit, start_state, lists)
        slab_share = lax.psum_scatter(target_sum, "rep", scatter_dimension=0, tiled=True)
        returned = returned + from_behind(slab_share, "blk", -(step + 1))
        operator_total = operator_total + lax.psum(operator_sum, ("blk", "rep"))
    entity_grad = lax.psum_scatter(source_sum, "rep", scatter_dimension=0, tiled=True) + returned
    return (entity_grad, operator_total)


def solution(mesh):
    return jax.shard_map(
        on_device,
        mesh=mesh,
        in_specs=(
            P("blk", None),
            P(),
            P(None, ("blk", "rep")),
            P(None, ("blk", "rep")),
            P(None, ("blk", "rep"), None),
            P(None, ("blk", "rep")),
            P(None, ("blk", "rep")),
        ),
        out_specs=(P(("blk", "rep"), None), P()),
        check_vma=False,
    )
```

profile of v0, /device:TPU:1, one launch (start us, length us, event | category | flops | bytes accessed | tf_op | source)
XLA Modules:
  0.0 599.1 jit_solution(9352732943776127317)
XLA Ops:
  8.0 2.1 collective-permute-start
  11.0 2.3 copy.39
  22.2 13.9 %collective-permute-done = bf16[1024,400]{0,1:T(8,128)(2,1)} collective-permute-done((bf16[1024,400]{0,1:T(8,128)(2,1)}, bf16[1024,400]{0,1:T(8,128)(2,1)}, u32[]{:S(2)}, u32[]{:S(2)}) %collective-permute-start) | collective-permute-done | bytes 819232 | tf_op jit(solution)/shard_map/ppermute | solution.py:10
  37.9 1.6 broadcast.195.clone
  39.5 119.9 %while.30 = (s32[]{:T(128)}, f32[1024,400]{1,0:T(8,128)}, f32[1024,400]{1,0:T(8,128)S(1)}, f32[2,400,400]{2,1,0:T(8,128)}, s32[2,500]{1,0:T(2,128)}, /*index=5*/...) while((s32[]{:T(128)}, f32[1024,400]{1,0:T(8,128)}, ...), condition=%wide.region_5.6_spmd.clone, body=%wide.region_0.5_spmd.clone.sunk | while | flops 1686472576 | bytes 41301436 | solution.py:88
  49.1 4.0 gather_fusion.1
  53.1 2.6 gather_fusion
  55.7 2.0 copy.54
  57.7 1.7 fusion.90
  61.8 2.5 copy.55
  64.3 5.3 gather_fusion.2
  69.6 2.3 multiply_convert_fusion.4
  73.5 2.0 fusion.94
  78.6 7.0 %scatter_fusion = f32[1024,400]{1,0:T(8,128)} fusion(f32[1024,400]{1,0:T(8,128)} %get-tuple-element.532, s32[500]{0:T(512)S(1)} %bitcast.151, f32[500,400]{1,0:T(8,128)} %fusion.93), kind=kCustom, calls=%fused_computation.6.clone.clone.1 | custom fusion | flops 200000 | bytes 2402000 | tf_op jit(solution)/shard_map/while/body/eval_jaxpr/scatter-add | solution.py:47
  85.6 5.0 scatter_fusion.1
  90.6 8.0 %scatter_fusion.2 = f32[1024,400]{1,0:T(8,128)S(1)} fusion(f32[1024,400]{1,0:T(8,128)S(1)} %scatter_fusion.1, s32[1000]{0:T(1024)S(1)} %bitcast.143, f32[1000,400]{1,0:T(8,128)} %fusion.94), kind=kCustom, calls=%fused_computation.8.clone.clone.1 | custom fusion | flops 400000 | bytes 4804000 | tf_op jit(solution)/shard_map/while/body/eval_jaxpr/scatter-add | solution.py:49
  108.2 4.0 gather_fusion.1
  112.3 2.6 gather_fusion
  114.9 2.0 copy.54
  116.8 1.7 fusion.90
  120.9 2.5 copy.55
  123.4 5.3 gather_fusion.2
  128.7 2.3 multiply_convert_fusion.4
  132.6 2.0 fusion.94
  136.2 3.0 select_add_fusion.4
  139.1 7.0 %scatter_fusion = f32[1024,400]{1,0:T(8,128)} fusion(f32[1024,400]{1,0:T(8,128)} %get-tuple-element.532, s32[500]{0:T(512)S(1)} %bitcast.151, f32[500,400]{1,0:T(8,128)} %fusion.93), kind=kCustom, calls=%fused_computation.6.clone.clone.1 | custom fusion | flops 200000 | bytes 2402000 | tf_op jit(solution)/shard_map/while/body/eval_jaxpr/scatter-add | solution.py:47
  146.2 5.0 scatter_fusion.1
  151.2 8.0 %scatter_fusion.2 = f32[1024,400]{1,0:T(8,128)S(1)} fusion(f32[1024,400]{1,0:T(8,128)S(1)} %scatter_fusion.1, s32[1000]{0:T(1024)S(1)} %bitcast.143, f32[1000,400]{1,0:T(8,128)} %fusion.94), kind=kCustom, calls=%fused_computation.8.clone.clone.1 | custom fusion | flops 400000 | bytes 4804000 | tf_op jit(solution)/shard_map/while/body/eval_jaxpr/scatter-add | solution.py:49
  159.4 1.7 copy.44
  162.9 118.9 %while.31 = (s32[]{:T(128)}, f32[1024,400]{1,0:T(8,128)}, f32[1024,400]{1,0:T(8,128)S(1)}, f32[2,400,400]{2,1,0:T(8,128)}, s32[2,500]{1,0:T(2,128)}, /*index=5*/...) while((s32[]{:T(128)}, f32[1024,400]{1,0:T(8,128)}, ...), condition=%wide.region_11.12_spmd.clone, body=%wide.region_6.0_spmd.clone.sunk | while | flops 1686472576 | bytes 41301436 | solution.py:88
  172.2 4.0 gather_fusion.4
  176.2 2.6 gather_fusion.3
  178.8 2.0 copy.56
  180.8 1.7 fusion.107
  184.7 2.5 copy.57
  187.2 5.3 gather_fusion.5
  192.5 2.3 multiply_convert_fusion.5
  196.4 2.0 fusion.111
  199.9 1.6 select_add_fusion.5
  201.5 7.1 %scatter_fusion.3 = f32[1024,400]{1,0:T(8,128)} fusion(f32[1024,400]{1,0:T(8,128)} %get-tuple-element.577, s32[500]{0:T(512)S(1)} %bitcast.153, f32[500,400]{1,0:T(8,128)} %fusion.110), kind=kCustom, calls=%fused_computation.9.clone.clone.1 | custom fusion | flops 200000 | bytes 2402000 | tf_op jit(solution)/shard_map/while/body/eval_jaxpr/scatter-add | solution.py:47
  208.6 5.0 scatter_fusion.4
  213.5 8.0 %scatter_fusion.5 = f32[1024,400]{1,0:T(8,128)S(1)} fusion(f32[1024,400]{1,0:T(8,128)S(1)} %scatter_fusion.4, s32[1000]{0:T(1024)S(1)} %bitcast.145, f32[1000,400]{1,0:T(8,128)} %fusion.111), kind=kCustom, calls=%fused_computation.11.clone.clone.1 | custom fusion | flops 400000 | bytes 4804000 | tf_op jit(solution)/shard_map/while/body/eval_jaxpr/scatter-add | solution.py:49
  230.8 4.0 gather_fusion.4
  234.8 2.6 gather_fusion.3
  237.4 2.0 copy.56
  239.4 1.7 fusion.107
  243.3 2.5 copy.57
  245.8 5.3 gather_fusion.5
  251.2 2.3 multiply_convert_fusion.5
  255.0 2.0 fusion.111
  258.5 3.0 select_add_fusion.5
  261.5 7.0 %scatter_fusion.3 = f32[1024,400]{1,0:T(8,128)} fusion(f32[1024,400]{1,0:T(8,128)} %get-tuple-element.577, s32[500]{0:T(512)S(1)} %bitcast.153, f32[500,400]{1,0:T(8,128)} %fusion.110), kind=kCustom, calls=%fused_computation.9.clone.clone.1 | custom fusion | flops 200000 | bytes 2402000 | tf_op jit(solution)/shard_map/while/body/eval_jaxpr/scatter-add | solution.py:47
  268.6 5.0 scatter_fusion.4
  273.5 8.0 %scatter_fusion.5 = f32[1024,400]{1,0:T(8,128)S(1)} fusion(f32[1024,400]{1,0:T(8,128)S(1)} %scatter_fusion.4, s32[1000]{0:T(1024)S(1)} %bitcast.145, f32[1000,400]{1,0:T(8,128)} %fusion.111), kind=kCustom, calls=%fused_computation.11.clone.clone.1 | custom fusion | flops 400000 | bytes 4804000 | tf_op jit(solution)/shard_map/while/body/eval_jaxpr/scatter-add | solution.py:49
  281.8 1.8 copy.45
  283.7 2.8 copy.43
  286.6 5.9 collective-permute-start.2
  292.5 32.3 %reduce-scatter.8.cloned.1.call-done = f32[256,400]{0,1:T(8,128)} async-done(((f32[1024,400]{0,1:T(8,128)}), f32[256,400]{0,1:T(8,128)}) %reduce-scatter.8.cloned.1.call-update) | async-done | bytes 409616 | tf_op jit(solution)/shard_map/reduce_scatter | solution.py:89
  324.7 5.2 collective-permute-start.3
  329.9 3.4 add.143
  333.4 34.3 %reduce-scatter.4.cloned.1.call-done = f32[256,400]{0,1:T(8,128)} async-done(((f32[1024,400]{0,1:T(8,128)}), f32[256,400]{0,1:T(8,128)}) %reduce-scatter.4.cloned.1.call-update) | async-done | bytes 409616 | tf_op jit(solution)/shard_map/reduce_scatter | solution.py:92
  367.8 1.8 add_add_fusion
  369.6 219.7 %all-reduce.2.cloned.1.call-done = f32[2,400,400]{2,1,0:T(8,128)} async-done(((f32[2,400,400]{2,1,0:T(8,128)}), f32[2,400,400]{2,1,0:T(8,128)}) %all-reduce.2.cloned.1.call-update) | async-done | bytes 1280016 | tf_op jit(solution)/shard_map/psum | solution.py:91
  589.3 2.7 copy.89
  (190 shorter events, 65.8 us)
Async XLA Ops:
  8.0 278.6 %reduce-scatter.6.cloned.1.call-start = ((), (), s32[]{:S(2)}) async-start(), calls=%async_computation.4 | async-start | bytes 2048000 | tf_op jit(solution)/shard_map/reduce_scatter | solution.py:89
  8.0 28.1 %collective-permute-start = (bf16[1024,400]{0,1:T(8,128)(2,1)}, bf16[1024,400]{0,1:T(8,128)(2,1)}, u32[]{:S(2)}, u32[]{:S(2)}) collective-permute-start(bf16[1024,400]{0,1:T(8,128)(2,1)} %param.11), channel_id=1, source_target_pairs={{252,0},{0,4},{4,8},{8,12},{12,16},{16,20},{20,24},{24,28},{28,32}... | collective-permute-start | bytes 2457608 | tf_op jit(solution)/shard_map/ppermute | solution.py:10
  36.2 125.0 %collective-permute-start.1 = (bf16[1024,400]{0,1:T(8,128)(2,1)}, bf16[1024,400]{0,1:T(8,128)(2,1)}, u32[]{:S(2)}, u32[]{:S(2)}) collective-permute-start(bf16[1024,400]{0,1:T(8,128)(2,1)} %collective-permute-done), channel_id=1, source_target_pairs={{252,0},{0,4},{4,8},{8,12},{12,16},{16,20},{20,24},{24,28},{28,32}... | collective-permute-start | bytes 2457608 | tf_op jit(solution)/shard_map/ppermute | solution.py:10
  47.2 1.3 copy-start.8
  47.9 0.5 copy-start.12
  47.9 0.6 copy-start.16
  60.1 0.6 copy-start.20
  69.6 2.3 copy-start.4
  69.6 2.3 copy-start.6
  69.6 2.3 copy-start.21
  71.9 1.0 copy-start
  73.5 2.0 copy-start.2
  73.5 3.6 copy-start.24
  77.0 1.6 copy-start.17
  78.6 7.0 %copy-start.13 = (s32[500,1]{0,1:T(1,128)S(1)}, s32[500,1]{0,1:T(1,128)}, u32[]{:S(2)}) copy-start(s32[500,1]{0,1:T(1,128)} %copy-done.12) | copy-start | bytes 6004 | tf_op jit(solution)/shard_map/while
  85.6 5.0 copy-start.9
  106.3 1.3 copy-start.8
  107.0 0.5 copy-start.12
  107.1 0.6 copy-start.16
  119.2 0.6 copy-start.20
  128.7 2.3 copy-start.4
  128.7 2.3 copy-start.6
  128.7 2.3 copy-start.21
  131.1 1.0 copy-start
  132.6 2.0 copy-start.2
  132.6 3.6 copy-start.24
  136.2 3.0 copy-start.17
  139.1 7.0 %copy-start.13 = (s32[500,1]{0,1:T(1,128)S(1)}, s32[500,1]{0,1:T(1,128)}, u32[]{:S(2)}) copy-start(s32[500,1]{0,1:T(1,128)} %copy-done.12) | copy-start | bytes 6004 | tf_op jit(solution)/shard_map/while
  146.2 5.0 copy-start.9
  161.2 163.6 %reduce-scatter.8.cloned.1.call-start = ((), (), s32[]{:S(2)}) async-start(), calls=%async_computation.5 | async-start | bytes 2048000 | tf_op jit(solution)/shard_map/reduce_scatter | solution.py:89
  170.3 1.3 copy-start.10
  171.0 0.5 copy-start.14
  171.0 0.5 copy-start.18
  183.1 0.6 copy-start.22
  192.5 2.3 copy-start.5
  192.5 2.3 copy-start.7
  192.5 2.3 copy-start.23
  194.9 1.1 copy-start.1
  196.4 2.0 copy-start.3
  196.4 3.5 copy-start.25
  199.9 1.6 copy-start.19
  201.5 7.1 %copy-start.15 = (s32[500,1]{0,1:T(1,128)S(1)}, s32[500,1]{0,1:T(1,128)}, u32[]{:S(2)}) copy-start(s32[500,1]{0,1:T(1,128)} %copy-done.14) | copy-start | bytes 6004 | tf_op jit(solution)/shard_map/while
  208.6 5.0 copy-start.11
  229.0 1.3 copy-start.10
  229.7 0.5 copy-start.14
  229.7 0.5 copy-start.18
  241.7 0.6 copy-start.22
  251.2 2.3 copy-start.5
  251.2 2.3 copy-start.7
  251.2 2.3 copy-start.23
  253.5 1.0 copy-start.1
  255.0 2.0 copy-start.3
  255.0 3.5 copy-start.25
  258.5 3.0 copy-start.19
  261.5 7.0 %copy-start.15 = (s32[500,1]{0,1:T(1,128)S(1)}, s32[500,1]{0,1:T(1,128)}, u32[]{:S(2)}) copy-start(s32[500,1]{0,1:T(1,128)} %copy-done.14) | copy-start | bytes 6004 | tf_op jit(solution)/shard_map/while
  268.6 5.0 copy-start.11
  283.6 84.1 %reduce-scatter.4.cloned.1.call-start = ((), (), s32[]{:S(2)}) async-start(), calls=%async_computation.3 | async-start | bytes 2048000 | tf_op jit(solution)/shard_map/reduce_scatter | solution.py:92
  286.5 302.8 %all-reduce.2.cloned.1.call-start = ((), (), s32[]{:S(2)}) async-start(), calls=%async_computation.6 | async-start | bytes 3276800 | tf_op jit(solution)/shard_map/psum | solution.py:91
  286.6 46.9 %collective-permute-start.2 = (f32[256,400]{0,1:T(8,128)}, f32[256,400]{0,1:T(8,128)S(1)}, u32[]{:S(2)}, u32[]{:S(2)}) collective-permute-start(f32[256,400]{0,1:T(8,128)} %reduce-scatter.6.cloned.1.call-done), channel_id=1, source_target_pairs={{4,0},{8,4},{12,8},{16,12},{20,16},{24,20},{28,24},{32,28},{36,32}... | collective-permute-start | bytes 1228808 | tf_op jit(solution)/shard_map/ppermute | solution.py:10
  324.7 43.0 %collective-permute-start.3 = (f32[256,400]{0,1:T(8,128)}, f32[256,400]{0,1:T(8,128)S(1)}, u32[]{:S(2)}, u32[]{:S(2)}) collective-permute-start(f32[256,400]{0,1:T(8,128)} %reduce-scatter.8.cloned.1.call-done), channel_id=1, source_target_pairs={{8,0},{12,4},{16,8},{20,12},{24,16},{28,20},{32,24},{36,28},{40,32... | collective-permute-start | bytes 1228808 | tf_op jit(solution)/shard_map/ppermute | solution.py:10
Sparse Core Ops, SparseCore 0:
  161.3 40.9 reduce-scatter.5
  283.8 40.9 reduce-scatter.7
  327.5 40.1 reduce-scatter.3
Sparse Core Ops, SparseCore 1:
  333.5 255.7 all-reduce.1
where the time goes:
time: 604 us; the launch traced here: 599 us
  waiting for transfers between devices  300 us (50%)
  other arithmetic  121 us (20%)
  local copies, waits for them, and re-layouts  105 us (17%)
  matrix products  34.5 us (6%)
  between operations  15.3 us (3%)
  starting transfers between devices  13.4 us (2%)
  loops' own time  8.95 us (1%)
    psum x1, waiting for transfers between devices, on_device(): operator_total = operator_total + lax.psum(operator_sum, ('blk', 'rep'))  220 us
    reduce_scatter x1, waiting for transfers between devices, on_device(): lax.psum_scatter(source_sum, 'rep', scatter_dimension=0, tiled=True)  34.3 us
    reduce_scatter x2, waiting for transfers between devices, on_device(): lax.psum_scatter(target_sum, 'rep', scatter_dimension=0, tiled=True)  32.3 us
    scatter-add x4, other arithmetic, account(): target_sum = target_sum.at[negative_rows].add(negative_rows_grad)  32.1 us
    scatter-add x4, other arithmetic, account(): source_sum = source_sum.at[source_rows].add(source_grad)  28.2 us
    gather x4, local copies, waits for them, and re-layouts, account(): negative_vectors = slab[negative_rows]  21.3 us
    scatter-add x4, other arithmetic, account(): target_sum.at[target_rows].add(positive_grad[:, None] * query_wide)  19.8 us
    gather x8, local copies, waits for them, and re-layouts, account(): target_vectors = slab[target_rows]  18.3 us
  transfers between devices with their start and end apart: 8, of which 4 were waited for; matrix products, arithmetic and copies ran while one was open for 42% of the time, Pallas kernels for 0%

commit v1 on v0

v1 whole, which is shorter than its diff:
```python
import functools

import jax
import jax.numpy as jnp
from jax import lax
from jax.experimental import pallas as pl
from jax.experimental.pallas import tpu as pltpu
from jax.sharding import PartitionSpec as P

MESH = pl.DeviceIdType.MESH
F32, BF16, I32 = jnp.float32, jnp.bfloat16, jnp.int32
PAD = 512
TILES = 80


def dot(a, b):
    return lax.dot_general(a, b, (((1,), (0,)), ((), ())), preferred_element_type=F32)


def dot_nt(a, b):
    return lax.dot_general(a, b, (((1,), (1,)), ((), ())), preferred_element_type=F32)


def eye(n):
    return (
        lax.broadcasted_iota(I32, (n, n), 0) == lax.broadcasted_iota(I32, (n, n), 1)
    ).astype(F32).astype(BF16)


def onehot(rows, base, index):
    shape = (rows, index.shape[1])
    return (lax.broadcasted_iota(I32, shape, 0) + base == index).astype(F32).astype(BF16)


def kernel(
    n_y, n_z, span, negs,
    emb, rel, src, tgt, neg, srel, ecnt,
    ent_out, rel_out,
    embt, opt, raw, lists, sel, ohs, svt, qt, cnt, slabt, slab, oht, ngm, cm, qhi, qlo, sgt,
    acc, acc_in, red, r1, s1, r2, s2, r3, g3, g2, g1, g_other,
    tsum, tsum_in, ret, ret_in, ssum, ssum_in, half, half_in,
    idx_s, idx_r, slab_s, slab_r, fwd_s, fwd_r, ar0_s, ar0_r, ar1_s, ar1_r, ar2_s, ar2_r, ar3_s, ar3_r,
    ag3_s, ag3_r, ag2_s, ag2_r, ag1_s, ag1_r, ag0_s, ag0_r, tx_s, tx_r, ret_s, ret_r, sx_s, sx_r, sy_s, sy_r,
):
    width = emb.shape[1]
    n_blk = 2 * n_y * n_z
    quarter = emb.shape[0] // 4
    b, r = lax.axis_index("blk"), lax.axis_index("rep")
    xh, core = r // 2, lax.rem(r, 2)
    xl, y, z = lax.rem(b, 2), lax.rem(b // 2, n_y), b // (2 * n_y)
    x = xh * 2 + xl
    sibling = (b, xh * 2 + 1 - core)
    mate = (b, (1 - xh) * 2 + core)

    def along_blk(k):
        return (lax.rem(b + k + n_blk, n_blk), r)

    def along_rep(k):
        return (b, lax.rem(r + k, 4))

    def x_at(k):
        return lax.rem(x + k, 4)

    def y_at(k):
        return lax.rem(y + k, n_y)

    def z_at(k):
        return lax.rem(z + k, n_z)

    def along_x(k):
        there = x_at(k)
        return ((z * n_y + y) * 2 + lax.rem(there, 2), (there // 2) * 2 + core)

    def along_y(k):
        return ((z * n_y + y_at(k)) * 2 + xl, r)

    def along_z(k):
        return ((z_at(k) * n_y + y) * 2 + xl, r)

    def send(source, target, sent, received, device):
        copy = pltpu.make_async_remote_copy(
            src_ref=source, dst_ref=target, send_sem=sent, recv_sem=received,
            device_id=device, device_id_type=MESH,
        )
        copy.start()
        return copy

    barrier = pltpu.get_barrier_semaphore()
    peers = [along_blk(k) for k in (1, 2, -1, -2)] + [along_rep(k) for k in (1, 2, 3)]
    peers += [along_x(k) for k in (1, 2, 3)] + [along_y(k) for k in range(1, n_y)]
    peers += [along_z(k) for k in range(1, n_z)]
    for peer in peers:
        pl.semaphore_signal(barrier, inc=1, device_id=peer, device_id_type=MESH)

    lane = lax.broadcasted_iota(I32, (8, 1024), 1)
    row = lax.broadcasted_iota(I32, (8, 1024), 0)
    raw[...] = jnp.zeros(raw.shape, I32)
    raw[0, 0:2, 0 : 2 * span] = src[...]
    raw[0, 2:4, 0 : 2 * span] = tgt[...]
    for s in range(2):
        raw[1, 2 * s : 2 * s + 2, 0:negs] = neg[s]
    edges = raw[0]
    second = pltpu.roll(edges, PAD - span, 1)
    edges = jnp.where(lane < PAD, edges, second)
    negatives = raw[1]
    packed = jnp.zeros((8, 1024), I32)
    for s in range(2):
        words = edges[s : s + 1] + edges[2 + s : 3 + s] * 65536
        packed = jnp.where(row == 4 * s, words, packed)
        words = negatives[2 * s : 2 * s + 1] + negatives[2 * s + 1 : 2 * s + 2] * 65536
        packed = jnp.where(row == 4 * s + 1, words, packed)
        for k in range(2):
            live = jnp.clip(ecnt[s, 0] - k * span, 0, span)
            packed = jnp.where(row == 4 * s + 2 + k, srel[s, k] + live * 65536, packed)
    lists[r] = packed

    unit = eye(width)
    for q in range(4):
        embt[q] = dot_nt(unit, emb[q * quarter : (q + 1) * quarter, :]).astype(BF16)
    for k in range(2):
        opt[k] = dot_nt(unit, rel[k]).astype(BF16)
    acc[...] = jnp.zeros(acc.shape, F32)
    s1[...] = jnp.zeros(s1.shape, F32)
    s2[...] = jnp.zeros(s2.shape, F32)

    pl.semaphore_wait(barrier, len(peers))

    index_copies = [
        send(lists.at[r], lists.at[r], idx_s.at[k - 1], idx_r.at[k - 1], along_rep(k))
        for k in (1, 2, 3)
    ]
    slab_copies = [
        send(embt.at[r], slabt.at[s, core], slab_s.at[s], slab_r.at[s], along_blk(s + 1))
        for s in range(2)
    ]
    for copy in index_copies:
        copy.wait()

    for s in range(2):
        before = jnp.zeros((1, 1024), I32)
        edge_words = [jnp.zeros((1, PAD), I32) for j in range(2)]
        negative_words = [jnp.zeros((1, 1024), I32) for j in range(2)]
        meta_words = [jnp.zeros((1, 1024), I32) for j in range(2)]
        for d in range(4):
            rows = lists[d]
            for k in range(2):
                meta = rows[4 * s + 2 + k : 4 * s + 3 + k]
                alive = (meta >= 65536).astype(I32)
                both = rows[4 * s + 1 : 4 * s + 2]
                negative = (both & 65535) if k == 0 else (both >> 16)
                edge = rows[4 * s : 4 * s + 1, k * PAD : (k + 1) * PAD]
                for j in range(2):
                    mine = alive * (before == 2 * core + j).astype(I32)
                    edge_words[j] += edge * mine[:, :PAD]
                    negative_words[j] += negative * mine
                    meta_words[j] += meta * mine
                before = before + alive
        lane1 = lax.broadcasted_iota(I32, (1, 1024), 1)
        for j in range(2):
            valid = lane1[:, :PAD] < (meta_words[j][:, :PAD] >> 16)
            at = 2 * s + j
            sel[at, 0:1, 0:PAD] = jnp.where(valid, edge_words[j] & 65535, -1)
            sel[at, 1:2, 0:PAD] = jnp.where(valid, edge_words[j] >> 16, -1)
            sel[at, 2:3, :] = jnp.where(lane1 < negs, negative_words[j], -1)
            sel[at, 3:4, :] = meta_words[j] & 1
            sel[at, 4:5, 0:PAD] = valid.astype(I32)

    def operator(table, at):
        second = sel[at, 3:4, 0:width].astype(F32)
        return (
            table[0].astype(F32) * (1.0 - second) + table[1].astype(F32) * second
        ).astype(BF16)

    def queries(s):
        def body(j, carry):
            at = 2 * s + j
            rows = sel[at, 0:1, 0:PAD]
            total = jnp.zeros((width, PAD), F32)
            for q in range(4):
                picked = onehot(quarter, q * quarter, rows)
                ohs[at, q] = picked
                total += dot(embt[q], picked)
            vectors = total.astype(BF16)
            svt[at] = vectors
            qt[at] = dot(operator(opt, at), vectors).astype(BF16)
            ones = jnp.ones((1024, 128), BF16)
            for h in range(2):
                cnt[at, h] = dot(onehot(quarter, (2 * xh + h) * quarter, sel[at, 2:3, :]), ones)
            return carry

        lax.fori_loop(0, 2, body, 0)

    def forward(s):
        slab_copies[s].wait_recv()
        return send(
            slabt.at[s, core], slabt.at[s, core], fwd_s.at[s], fwd_r.at[s], sibling
        )

    chunk = 128

    def score(s):
        turn = eye(quarter)
        for h in range(2):
            slab[h] = dot_nt(turn, slabt[s, h]).astype(BF16)

        def body(j, carry):
            at = 2 * s + j
            rows = sel[at, 1:2, 0:PAD]
            live = sel[at, 4:5, 0:PAD].astype(F32)
            for h in range(2):
                oht[h] = onehot(quarter, (2 * xh + h) * quarter, rows)
            target = dot(slabt[s, 0], oht[0]) + dot(slabt[s, 1], oht[1])
            positive = jnp.sum(qt[at].astype(F32) * target, axis=0, keepdims=True)
            positive_grad = -live * jax.nn.sigmoid(-positive)
            weight = live * (negs**-0.5)

            def part(i, carry):
                h, at_row = i // (quarter // chunk), lax.rem(i, quarter // chunk) * chunk
                here = pl.ds(pl.multiple_of(at_row, chunk), chunk)
                scores = dot(slab[h, here, :], qt[at])
                times = cnt[at, h, here, :]
                times = jnp.concatenate([times] * (PAD // 128), axis=1)
                grad = (jax.nn.sigmoid(scores) * (times * weight)).astype(BF16)
                ngm[h, here, :] = grad
                mark = oht[h, here, :].astype(F32)
                cm[at, h, here, :] = (grad.astype(F32) + mark * positive_grad).astype(BF16)
                return carry

            lax.fori_loop(0, 2 * (quarter // chunk), part, 0)
            grad = positive_grad * target + dot(slabt[s, 0], ngm[0]) + dot(slabt[s, 1], ngm[1])
            high = grad.astype(BF16)
            low = (grad - high.astype(F32)).astype(BF16)
            qhi[at] = high
            qlo[at] = low
            vectors = svt[at]
            main = dot_nt(vectors, qhi[at, 0:384]) + dot_nt(vectors, qlo[at, 0:384])
            rest = dot_nt(qhi[at, 384:width], vectors) + dot_nt(qlo[at, 384:width], vectors)
            rest = jnp.concatenate([rest, jnp.zeros((16, PAD - width), F32)], axis=1)
            second = sel[at, 3:4, 0:128].astype(F32).reshape(1, 1, 128)
            n = width // 16
            for k, share in ((0, 1.0 - second), (1, second)):
                for t in range(3):
                    tiles = main[:, 128 * t : 128 * t + 128].reshape(n, 16, 128)
                    acc[k, n * t : n * t + n] += tiles * share
                for t in range(4):
                    acc[k, 3 * n + t] += rest[:, 128 * t : 128 * t + 128] * share[0]
            return carry

        lax.fori_loop(0, 2, body, 0)

    queries(0)
    forwards = [forward(0)]
    queries(1)
    forwards.append(forward(1))
    forwards[0].wait_recv()
    score(0)
    forwards[1].wait_recv()
    score(1)

    copy0 = send(acc.at[1 - core], acc_in, ar0_s, ar0_r, sibling)

    def target_sums(i, carry):
        s, h = i // 2, lax.rem(i, 2)
        tsum[s, h] = dot_nt(qt[2 * s], cm[2 * s, h]) + dot_nt(qt[2 * s + 1], cm[2 * s + 1, h])
        return carry

    lax.fori_loop(0, 4, target_sums, 0)
    tx_copies = [
        send(tsum.at[s, 1 - core], tsum_in.at[s], tx_s.at[s], tx_r.at[s], sibling)
        for s in range(2)
    ]

    copy0.wait_recv()
    red[...] = acc[core] + acc_in[...]
    r1[0, x] = red[pl.ds(10 * x, 10)]
    r1[1, y] = red[pl.ds(40 + 10 * y, 10)]
    copies1 = []
    for k in range(1, 4):
        copies1.append(
            send(red.at[pl.ds(10 * x_at(k), 10)], r1.at[0, x], ar1_s.at[0, k - 1], ar1_r.at[0, k - 1], along_x(k))
        )
        copies1.append(
            send(red.at[pl.ds(40 + 10 * y_at(k), 10)], r1.at[1, y], ar1_s.at[1, k - 1], ar1_r.at[1, k - 1], along_y(k))
        )

    def source_vectors(at, carry):
        turned = operator(rel, at)
        sgt[at] = (dot(turned, qhi[at]) + dot(turned, qlo[at])).astype(BF16)
        return carry

    lax.fori_loop(0, 4, source_vectors, 0)

    def source_sums(q, carry):
        total = dot_nt(sgt[0], ohs[0, q])
        for at in range(1, 4):
            total += dot_nt(sgt[at], ohs[at, q])
        ssum[q // 2, lax.rem(q, 2)] = total
        return carry

    lax.fori_loop(0, 4, source_sums, 0)
    sx_copies = [
        send(ssum.at[h, 1 - core], ssum_in.at[h], sx_s.at[h], sx_r.at[h], sibling)
        for h in range(2)
    ]

    for copy in copies1:
        copy.wait_recv()
    for h in range(2):
        s1[h, 0:10] = (r1[h, 0] + r1[h, 1]) + (r1[h, 2] + r1[h, 3])
    r2[0, y] = s1[0, pl.ds(3 * y, 3)]
    r2[1, x] = s1[1, pl.ds(3 * x, 3)]
    copies2 = []
    for k in range(1, 4):
        copies2.append(
            send(s1.at[0, pl.ds(3 * y_at(k), 3)], r2.at[0, y], ar2_s.at[0, k - 1], ar2_r.at[0, k - 1], along_y(k))
        )
        copies2.append(
            send(s1.at[1, pl.ds(3 * x_at(k), 3)], r2.at[1, x], ar2_s.at[1, k - 1], ar2_r.at[1, k - 1], along_x(k))
        )

    ret_copies = []
    for s in range(2):
        tx_copies[s].wait_recv()
        ret[s] = (tsum[s, core] + tsum_in[s]).astype(BF16)
        ret_copies.append(
            send(ret.at[s], ret_in.at[s], ret_s.at[s], ret_r.at[s], along_blk(-(s + 1)))
        )

    for copy in copies2:
        copy.wait_recv()
    for h in range(2):
        s2[3 * h : 3 * h + 3] = (r2[h, 0] + r2[h, 1]) + (r2[h, 2] + r2[h, 3])
    r3[z] = s2[z]
    copies3 = [
        send(s2.at[z_at(k)], r3.at[z], ar3_s.at[k - 1], ar3_r.at[k - 1], along_z(k))
        for k in range(1, n_z)
    ]

    for copy in sx_copies:
        copy.wait_recv()
    half[...] = (ssum[1 - xh, core] + ssum_in[1 - xh]).astype(BF16)
    sy_copy = send(half, half_in, sy_s, sy_r, mate)

    for copy in copies3:
        copy.wait_recv()
    total = r3[0]
    for k in range(1, n_z):
        total += r3[k]
    g3[z] = total.astype(BF16)
    copies = [
        send(g3.at[z], g3.at[z], ag3_s.at[k - 1], ag3_r.at[k - 1], along_z(k))
        for k in range(1, n_z)
    ]
    sends = list(copies)
    for copy in copies:
        copy.wait_recv()
    g2[0, y] = g3[0:3]
    g2[1, x] = g3[3:6]
    copies = []
    for k in range(1, 4):
        copies.append(send(g2.at[0, y], g2.at[0, y], ag2_s.at[0, k - 1], ag2_r.at[0, k - 1], along_y(k)))
        copies.append(send(g2.at[1, x], g2.at[1, x], ag2_s.at[1, k - 1], ag2_r.at[1, k - 1], along_x(k)))
    sends += copies
    for copy in copies:
        copy.wait_recv()
    for h, at in ((0, x), (1, y)):
        for k in range(3):
            g1[h, at, 3 * k : 3 * k + 3] = g2[h, k]
        g1[h, at, 9] = g2[h, 3, 0]
    copies = []
    for k in range(1, 4):
        copies.append(send(g1.at[0, x], g1.at[0, x], ag1_s.at[0, k - 1], ag1_r.at[0, k - 1], along_x(k)))
        copies.append(send(g1.at[1, y], g1.at[1, y], ag1_s.at[1, k - 1], ag1_r.at[1, k - 1], along_y(k)))
    sends += copies

    sy_copy.wait_recv()
    for copy in ret_copies:
        copy.wait_recv()
    total = (ssum[xh, core] + ssum_in[xh]) + half_in[...].astype(F32)
    total = total + (ret_in[0].astype(F32) + ret_in[1].astype(F32))
    total = jnp.concatenate([total, jnp.zeros((PAD - width, quarter), F32)], axis=0)
    ent_out[...] = total.T[:, :width]

    for copy in copies:
        copy.wait_recv()
    copy = send(g1, g_other, ag0_s, ag0_r, sibling)
    sends.append(copy)

    def write(k, tiles):
        n = width // 16
        for t in range(3):
            rel_out[k, :, 128 * t : 128 * t + 128] = (
                tiles[n * t : n * t + n].astype(F32).reshape(width, 128)
            )
        rest = jnp.concatenate([tiles[3 * n + t].astype(F32) for t in range(4)], axis=1)
        rest = jnp.concatenate([rest, jnp.zeros((112, PAD), F32)], axis=0)
        rel_out[k, :, 384:width] = rest.T[:width, : width - 384]

    write(core, g1[...].reshape(TILES, 16, 128))
    copy.wait_recv()
    write(1 - core, g_other[...].reshape(TILES, 16, 128))

    for copy in slab_copies + forwards + [copy0, sy_copy]:
        copy.wait_send()
    for copy in tx_copies + copies1 + copies2 + copies3 + sx_copies + ret_copies + sends:
        copy.wait_send()


def on_device(n_y, n_z, embeddings, relations, *lists):
    rows, width = embeddings.shape
    quarter = rows // 4
    span = lists[0].shape[1] // 2
    negs = lists[2].shape[2]
    dma = pltpu.SemaphoreType.DMA
    vmem, smem = pl.BlockSpec(memory_space=pltpu.VMEM), pl.BlockSpec(memory_space=pltpu.SMEM)

    def buffer(*shape, kind=F32):
        return pltpu.VMEM(shape, kind)

    scratch = [
        buffer(4, width, quarter, kind=BF16),
        buffer(2, width, width, kind=BF16),
        buffer(2, 8, 1024, kind=I32),
        buffer(4, 8, 1024, kind=I32),
        buffer(4, 8, 1024, kind=I32),
        buffer(4, 4, quarter, PAD, kind=BF16),
        buffer(4, width, PAD, kind=BF16),
        buffer(4, width, PAD, kind=BF16),
        buffer(4, 2, quarter, 128),
        buffer(2, 2, width, quarter, kind=BF16),
        buffer(2, quarter, width, kind=BF16),
        buffer(2, quarter, PAD, kind=BF16),
        buffer(2, quarter, PAD, kind=BF16),
        buffer(4, 2, quarter, PAD, kind=BF16),
        buffer(4, width, PAD, kind=BF16),
        buffer(4, width, PAD, kind=BF16),
        buffer(4, width, PAD, kind=BF16),
        buffer(2, TILES, 16, 128),
        buffer(TILES, 16, 128),
        buffer(TILES, 16, 128),
        buffer(2, 4, 10, 16, 128),
        buffer(2, 12, 16, 128),
        buffer(2, 4, 3, 16, 128),
        buffer(8, 16, 128),
        buffer(8, 16, 128),
        buffer(8, 16, 128, kind=BF16),
        buffer(2, 4, 3, 16, 128, kind=BF16),
        buffer(2, 4, 10, 16, 128, kind=BF16),
        buffer(2, 4, 10, 16, 128, kind=BF16),
        buffer(2, 2, width, quarter),
        buffer(2, width, quarter),
        buffer(2, width, quarter, kind=BF16),
        buffer(2, width, quarter, kind=BF16),
        buffer(2, 2, width, quarter),
        buffer(2, width, quarter),
        buffer(width, quarter, kind=BF16),
        buffer(width, quarter, kind=BF16),
    ]
    for shape in (
        (3,), (2,), (2,), None, (2, 3), (2, 3), (n_z - 1,),
        (n_z - 1,), (2, 3), (2, 3), None, (2,), (2,), (2,), None,
    ):
        scratch += [dma if shape is None else dma(shape)] * 2
    return pl.pallas_call(
        functools.partial(kernel, n_y, n_z, span, negs),
        out_shape=(
            jax.ShapeDtypeStruct((quarter, width), F32),
            jax.ShapeDtypeStruct(relations.shape, F32),
        ),
        in_specs=[vmem] * 5 + [smem] * 2,
        out_specs=(vmem, vmem),
        scratch_shapes=scratch,
        compiler_params=pltpu.CompilerParams(
            collective_id=0, has_side_effects=True, vmem_limit_bytes=56 * 2**20
        ),
    )(embeddings, relations, *lists)


def solution(mesh):
    n_y = 4
    n_z = mesh.shape["blk"] // (2 * n_y)
    return jax.shard_map(
        functools.partial(on_device, n_y, n_z),
        mesh=mesh,
        in_specs=(
            P("blk", None),
            P(),
            P(None, ("blk", "rep")),
            P(None, ("blk", "rep")),
            P(None, ("blk", "rep"), None),
            P(None, ("blk", "rep")),
            P(None, ("blk", "rep")),
        ),
        out_specs=(P(("blk", "rep"), None), P()),
        check_vma=False,
    )
```

time: 604 us -> 86.5 us (0.14)
  waiting for transfers between devices: 300 us -> 0 us
  other arithmetic: 121 us -> 0 us
  local copies, waits for them, and re-layouts: 105 us -> 8.2 us
  Pallas kernels: 0 us -> 77.4 us
  matrix products: 34.5 us -> 0 us
  between operations: 15.3 us -> 0.64 us
  starting transfers between devices: 13.4 us -> 0 us
  loops' own time: 8.95 us -> 0 us
    psum x1 -> x0, waiting for transfers between devices: 220 us -> none  [on_device(): operator_total = operator_total + lax.psum(operator_sum, ('blk', 'rep'))]
    scatter-add x12 -> x0, other arithmetic: 80.1 us -> none  [the longest x4 32.1 us: account(): target_sum = target_sum.at[negative_rows].add(negative_rows_grad)]
    pallas_call x0 -> x1, Pallas kernels: none -> 77.4 us  [on_device(): pl.pallas_call(functools.partial(kernel, n_y, n_z, span, negs), out_shape...]
    reduce_scatter x3 -> x0, waiting for transfers between devices: 66.6 us -> none  [the longest x1 34.3 us: on_device(): lax.psum_scatter(source_sum, 'rep', scatter_dimension=0, tiled=True)]
    gather x16 -> x0, local copies, waits for them, and re-layouts: 55.7 us -> none  [the longest x4 21.3 us: account(): negative_vectors = slab[negative_rows]]
    dot_general x24 -> x0, matrix products: 34.5 us -> none  [the longest x4 9.16 us: account(): lax.dot_general(query, negative_vectors, (((1,), (1,)), ((), ())), prefer...]
    add x6 -> x0, other arithmetic: 14.4 us -> none  [the longest x4 9.11 us: account(): operator_sum = operator_sum + selector[:, None, None] * operator_grad]
    ppermute x4 -> x0, waiting for transfers between devices: 13.9 us -> none  [from_behind(): return lax.ppermute(block, axis, route)]
  transfers between devices with their start and end apart: 8 -> 0, of which waited for: 4 -> 0; matrix products, arithmetic and copies ran while one was open for 42% -> 0% of each run, Pallas kernels for 0% -> 0%
where the time goes in v1:
time: 86.5 us; the launch traced here: 86.3 us
  Pallas kernels  77.4 us (89%)
  local copies, waits for them, and re-layouts  8.2 us (9%)
    pallas_call x1, Pallas kernels, on_device(): pl.pallas_call(functools.partial(kernel, n_y, n_z, span, negs), out_shape...  77.4 us
    unnamed x3, local copies, waits for them, and re-layouts  6.24 us
    pallas_call x1, local copies, waits for them, and re-layouts, on_device(): pl.pallas_call(functools.partial(kernel, n_y, n_z, span, negs), out_shape...  1.97 us

profile of v1, /device:TPU:1, one launch (start us, length us, event | category | flops | bytes accessed | tf_op | source)
XLA Modules:
  0.0 86.3 jit_solution(4129968632595593461)
XLA Ops:
  0.6 1.3 %copy.10.ecnt = s32[2,1]{1,0:T(2,128)} copy(s32[2,1]{0,1:T(1,128)} %param.13) | data formatting | bytes 16 | tf_op args[6]
  1.9 2.2 %copy.9.emb = bf16[1024,400]{1,0:T(8,128)(2,1)} copy(bf16[1024,400]{0,1:T(8,128)(2,1)} %param.7) | data formatting | bytes 1638400 | tf_op args[0]
  4.2 77.4 %shard_map.86 = (f32[256,400]{1,0:T(8,128)}, f32[2,400,400]{2,1,0:T(8,128)}) custom-call(bf16[1024,400]{1,0:T(8,128)(2,1)} %copy.9.emb, bf16[2,400,400]{2,1,0:T(8,128)(2,1)} %rel.1, s32[2,1000]{1,0:T(2,128)} %src.1, s32[2,1000]{1,0:T(2,128)} %tgt.1, s32[2,2,1000]{2,1,0:T(2,128)} %neg.1, s32[2,2]{1,0:T(2,128)} %srel.1, s32[2,1]{1,0:T(2,128)} %copy.10.ecnt), custom_call_target="tpu_custom_call" | custom-call | tf_op jit(solution)/shard_map/pallas_call | solution.py:464
  81.6 2.0 %copy.11 = f32[256,400]{0,1:T(8,128)} copy(f32[256,400]{1,0:T(8,128)} %get-tuple-element.2) | data formatting | bytes 819200 | tf_op jit(solution)/shard_map/pallas_call | solution.py:464
  83.5 2.7 %copy.13 = f32[2,400,400]{2,1,0:T(8,128)} copy(f32[2,400,400]{2,1,0:T(8,128)} %get-tuple-element.7) | data formatting | bytes 2560000

commit v2 on v1

v2 whole, which is shorter than its diff:
```python
import functools

import jax
import jax.numpy as jnp
from jax import lax
from jax.experimental import pallas as pl
from jax.experimental.pallas import tpu as pltpu
from jax.sharding import PartitionSpec as P

MESH = pl.DeviceIdType.MESH
F32, BF16, I32 = jnp.float32, jnp.bfloat16, jnp.int32
PAD = 512
TILES = 80


def dot(a, b):
    return lax.dot_general(a, b, (((1,), (0,)), ((), ())), preferred_element_type=F32)


def dot_nt(a, b):
    return lax.dot_general(a, b, (((1,), (1,)), ((), ())), preferred_element_type=F32)


def eye(n):
    return (
        lax.broadcasted_iota(I32, (n, n), 0) == lax.broadcasted_iota(I32, (n, n), 1)
    ).astype(F32).astype(BF16)


def onehot(rows, base, index):
    shape = (rows, index.shape[1])
    return (lax.broadcasted_iota(I32, shape, 0) + base == index).astype(F32).astype(BF16)


def kernel(
    n_y, n_z, span, negs,
    emb, rel, src, tgt, neg, srel, ecnt,
    ent_out, rel_out,
    opt, raw, lists, sel, ohs, svt, qt, cnt, slabt, slab, oht, ngm, pgs, qhl, sgt,
    acc, acc_in, red, r1, s1, r2, zx, g2, g1, g_other,
    tsum, tsum_in, ret, ret_in, ssum, ssum_in, half, half_in,
    idx_s, idx_r, slab_s, slab_r, fwd_s, fwd_r, ar0_s, ar0_r, ar1_s, ar1_r, ar2_s, ar2_r, ar3_s, ar3_r,
    ag2_s, ag2_r, ag1_s, ag1_r, ag0_s, ag0_r, tx_s, tx_r, ret_s, ret_r, sx_s, sx_r, sy_s, sy_r,
):
    width = emb.shape[0]
    n_blk = 2 * n_y * n_z
    quarter = emb.shape[1] // 4
    b, r = lax.axis_index("blk"), lax.axis_index("rep")
    xh, core = r // 2, lax.rem(r, 2)
    xl, y, z = lax.rem(b, 2), lax.rem(b // 2, n_y), b // (2 * n_y)
    x = xh * 2 + xl
    sibling = (b, xh * 2 + 1 - core)
    mate = (b, (1 - xh) * 2 + core)

    def along_blk(k):
        return (lax.rem(b + k + n_blk, n_blk), r)

    def along_rep(k):
        return (b, lax.rem(r + k, 4))

    def x_at(k):
        return lax.rem(x + k, 4)

    def y_at(k):
        return lax.rem(y + k, n_y)

    def z_at(k):
        return lax.rem(z + k, n_z)

    def along_x(k):
        there = x_at(k)
        return ((z * n_y + y) * 2 + lax.rem(there, 2), (there // 2) * 2 + core)

    def along_y(k):
        return ((z * n_y + y_at(k)) * 2 + xl, r)

    def along_z(k):
        return ((z_at(k) * n_y + y) * 2 + xl, r)

    def send(source, target, sent, received, device):
        copy = pltpu.make_async_remote_copy(
            src_ref=source, dst_ref=target, send_sem=sent, recv_sem=received,
            device_id=device, device_id_type=MESH,
        )
        copy.start()
        return copy

    barrier = pltpu.get_barrier_semaphore()
    peers = [along_blk(k) for k in (1, 2, -1, -2)] + [along_rep(k) for k in (1, 2, 3)]
    peers += [along_x(k) for k in (1, 2, 3)] + [along_y(k) for k in range(1, n_y)]
    peers += [along_z(k) for k in range(1, n_z)]
    for peer in peers:
        pl.semaphore_signal(barrier, inc=1, device_id=peer, device_id_type=MESH)

    lane = lax.broadcasted_iota(I32, (8, 1024), 1)
    row = lax.broadcasted_iota(I32, (8, 1024), 0)
    raw[...] = jnp.zeros(raw.shape, I32)
    raw[0, 0:2, 0 : 2 * span] = src[...]
    raw[0, 2:4, 0 : 2 * span] = tgt[...]
    for s in range(2):
        raw[1, 2 * s : 2 * s + 2, 0:negs] = neg[s]
    edges = raw[0]
    second = pltpu.roll(edges, PAD - span, 1)
    edges = jnp.where(lane < PAD, edges, second)
    negatives = raw[1]
    packed = jnp.zeros((8, 1024), I32)
    for s in range(2):
        words = edges[s : s + 1] + edges[2 + s : 3 + s] * 65536
        packed = jnp.where(row == 4 * s, words, packed)
        words = negatives[2 * s : 2 * s + 1] + negatives[2 * s + 1 : 2 * s + 2] * 65536
        packed = jnp.where(row == 4 * s + 1, words, packed)
        for k in range(2):
            live = jnp.clip(ecnt[0, s] - k * span, 0, span)
            packed = jnp.where(row == 4 * s + 2 + k, srel[s, k] + live * 65536, packed)
    lists[r] = packed

    pl.semaphore_wait(barrier, len(peers))

    index_copies = [
        send(lists.at[r], lists.at[r], idx_s.at[k - 1], idx_r.at[k - 1], along_rep(k))
        for k in (1, 2, 3)
    ]
    slab_copies = [
        send(emb.at[:, pl.ds(pl.multiple_of(r * quarter, quarter), quarter)], slabt.at[s, core], slab_s.at[s], slab_r.at[s], along_blk(s + 1))
        for s in range(2)
    ]

    unit = eye(width)
    for k in range(2):
        opt[k] = dot_nt(unit, rel[k]).astype(BF16)
    s1[...] = jnp.zeros(s1.shape, F32)
    for copy in index_copies:
        copy.wait()

    for s in range(2):
        before = jnp.zeros((1, 1024), I32)
        edge_words = [jnp.zeros((1, PAD), I32) for j in range(2)]
        negative_words = [jnp.zeros((1, 1024), I32) for j in range(2)]
        meta_words = [jnp.zeros((1, 1024), I32) for j in range(2)]
        for d in range(4):
            rows = lists[d]
            for k in range(2):
                meta = rows[4 * s + 2 + k : 4 * s + 3 + k]
                alive = (meta >= 65536).astype(I32)
                both = rows[4 * s + 1 : 4 * s + 2]
                negative = (both & 65535) if k == 0 else (both >> 16)
                edge = rows[4 * s : 4 * s + 1, k * PAD : (k + 1) * PAD]
                for j in range(2):
                    mine = alive * (before == 2 * core + j).astype(I32)
                    edge_words[j] += edge * mine[:, :PAD]
                    negative_words[j] += negative * mine
                    meta_words[j] += meta * mine
                before = before + alive
        lane1 = lax.broadcasted_iota(I32, (1, 1024), 1)
        for j in range(2):
            valid = lane1[:, :PAD] < (meta_words[j][:, :PAD] >> 16)
            at = 2 * s + j
            sel[at, 0:1, 0:PAD] = jnp.where(valid, edge_words[j] & 65535, -1)
            sel[at, 1:2, 0:PAD] = jnp.where(valid, edge_words[j] >> 16, -1)
            sel[at, 2:3, :] = jnp.where(lane1 < negs, negative_words[j], -1)
            sel[at, 3:4, :] = meta_words[j] & 1
            sel[at, 4:5, 0:PAD] = valid.astype(I32)

    def operator(table, at):
        second = sel[at, 3:4, 0:width].astype(F32)
        return (
            table[0].astype(F32) * (1.0 - second) + table[1].astype(F32) * second
        ).astype(BF16)

    def queries(s):
        for j in range(2):
            at = 2 * s + j
            ohs[at] = onehot(4 * quarter, 0, sel[at, 0:1, 0:PAD])
            vectors = dot(emb[...], ohs[at]).astype(BF16)
            svt[at] = vectors
            qt[at] = dot(operator(opt, at), vectors).astype(BF16)
            times = dot(onehot(2 * quarter, 2 * xh * quarter, sel[at, 2:3, :]), jnp.ones((1024, 128), BF16))
            cnt[at] = times * (0.5 * negs**-0.5)

    def forward(s):
        slab_copies[s].wait_recv()
        return send(
            slabt.at[s, core], slabt.at[s, core], fwd_s.at[s], fwd_r.at[s], sibling
        )

    def score(s):
        turn = eye(quarter) * jnp.asarray(0.5, BF16)
        for h in range(2):
            slab[h * quarter : (h + 1) * quarter] = dot_nt(turn, slabt[s, h]).astype(BF16)
        turned = jnp.concatenate([slabt[s, 0], slabt[s, 1]], axis=1)
        mains, rests, seconds = [], [], []
        for j in range(2):
            at = 2 * s + j
            oht[at] = onehot(2 * quarter, 2 * xh * quarter, sel[at, 1:2, 0:PAD])
            query = qt[at]
            target = dot(turned, oht[at])
            positive = jnp.sum(query.astype(F32) * target, axis=0, keepdims=True)
            positive_grad = -sel[at, 4:5, 0:PAD].astype(F32) * jax.nn.sigmoid(-positive)
            pgs[at, 0:1] = positive_grad
            for i in range(0, 2 * quarter, 128):
                bent = jnp.tanh(dot(slab[i : i + 128], query))
                times = jnp.concatenate([cnt[at, i : i + 128]] * (PAD // 128), axis=1)
                ngm[at, i : i + 128] = (times * bent + times).astype(BF16)
            grad = positive_grad * target + dot(turned, ngm[at])
            high = grad.astype(BF16)
            qhl[at, :, 0:PAD] = high
            qhl[at, :, PAD:] = (grad - high.astype(F32)).astype(BF16)
            vectors = jnp.concatenate([svt[at]] * 2, axis=1)
            mains.append(dot_nt(vectors, qhl[at, 0:384]))
            rest = dot_nt(qhl[at, 384:width], vectors)
            rests.append(jnp.concatenate([rest, jnp.zeros((16, PAD - width), F32)], axis=1))
            seconds.append(sel[at, 3:4, 0:128].astype(F32))
        n = width // 16
        for k in range(2):
            shares = [second if k else 1.0 - second for second in seconds]
            for t in range(3):
                tiles = sum(
                    main[:, 128 * t : 128 * t + 128] * share for main, share in zip(mains, shares)
                ).reshape(n, 16, 128)
                acc[k, n * t : n * t + n] = tiles if s == 0 else acc[k, n * t : n * t + n] + tiles
            for t in range(4):
                tile = sum(
                    rest[:, 128 * t : 128 * t + 128] * share for rest, share in zip(rests, shares)
                )
                acc[k, 3 * n + t] = tile if s == 0 else acc[k, 3 * n + t] + tile
            if s == 0:
                acc[k, 3 * n + 4] = jnp.zeros((16, 128), F32)

    queries(0)
    queries(1)
    forwards = [forward(0)]
    forwards[0].wait_recv()
    score(0)
    forwards.append(forward(1))
    forwards[1].wait_recv()
    score(1)

    copy0 = send(acc.at[1 - core], acc_in, ar0_s, ar0_r, sibling)
    copy0.wait_recv()
    red[...] = acc[core] + acc_in[...]
    r1[0, x] = red[pl.ds(10 * x, 10)]
    r1[1, y] = red[pl.ds(40 + 10 * y, 10)]
    copies1 = []
    for k in (2, 1, 3):
        copies1.append(
            send(red.at[pl.ds(10 * x_at(k), 10)], r1.at[0, x], ar1_s.at[0, k - 1], ar1_r.at[0, k - 1], along_x(k))
        )
        copies1.append(
            send(red.at[pl.ds(40 + 10 * y_at(k), 10)], r1.at[1, y], ar1_s.at[1, k - 1], ar1_r.at[1, k - 1], along_y(k))
        )

    for s in range(2):
        positives = [(pgs[at, 0:1] * qt[at].astype(F32)).astype(BF16) for at in (2 * s, 2 * s + 1)]
        left = jnp.concatenate([qt[2 * s], qt[2 * s + 1]] + positives, axis=1)
        for h in range(2):
            rows = slice(h * quarter, (h + 1) * quarter)
            parts = [ngm[2 * s, rows], ngm[2 * s + 1, rows], oht[2 * s, rows], oht[2 * s + 1, rows]]
            tsum[s, h] = dot_nt(left, jnp.concatenate(parts, axis=1))
    tx_copies = [
        send(tsum.at[s, 1 - core], tsum_in.at[s], tx_s.at[s], tx_r.at[s], sibling)
        for s in range(2)
    ]

    for at in range(4):
        turned = operator(rel, at)
        both = jnp.concatenate([qhl[at, :, 0:PAD], qhl[at, :, PAD:]], axis=0)
        sgt[at] = dot(jnp.concatenate([turned, turned], axis=1), both).astype(BF16)

    left = jnp.concatenate([sgt[at] for at in range(4)], axis=1)
    for q in range(4):
        rows = slice(q * quarter, (q + 1) * quarter)
        ssum[q // 2, q % 2] = dot_nt(left, jnp.concatenate([ohs[at, rows] for at in range(4)], axis=1))
    sx_copies = [
        send(ssum.at[h, 1 - core], ssum_in.at[h], sx_s.at[h], sx_r.at[h], sibling)
        for h in range(2)
    ]

    for copy in copies1:
        copy.wait_recv()
    for h in range(2):
        s1[h, 0:10] = (r1[h, 0] + r1[h, 1]) + (r1[h, 2] + r1[h, 3])
    r2[0, y] = s1[0, pl.ds(3 * y, 3)]
    r2[1, x] = s1[1, pl.ds(3 * x, 3)]
    copies2 = []
    for k in range(1, 4):
        copies2.append(
            send(s1.at[0, pl.ds(3 * y_at(k), 3)], r2.at[0, y], ar2_s.at[0, k - 1], ar2_r.at[0, k - 1], along_y(k))
        )
        copies2.append(
            send(s1.at[1, pl.ds(3 * x_at(k), 3)], r2.at[1, x], ar2_s.at[1, k - 1], ar2_r.at[1, k - 1], along_x(k))
        )

    for copy in copies2:
        copy.wait_recv()
    for h in range(2):
        total = (r2[h, 0] + r2[h, 1]) + (r2[h, 2] + r2[h, 3])
        zx[z, 3 * h : 3 * h + 3] = total.astype(BF16)
    copies3 = [
        send(zx.at[z], zx.at[z], ar3_s.at[k - 1], ar3_r.at[k - 1], along_z(k))
        for k in sorted(range(1, n_z), key=lambda k: -min(k, n_z - k))
    ]

    for copy in sx_copies:
        copy.wait_recv()
    half[...] = (ssum[1 - xh, core] + ssum_in[1 - xh]).astype(BF16)
    sy_copy = send(half, half_in, sy_s, sy_r, mate)
    ret_copies = []
    for s in range(2):
        tx_copies[s].wait_recv()
        ret[s] = (tsum[s, core] + tsum_in[s]).astype(BF16)
        ret_copies.append(
            send(ret.at[s], ret_in.at[s], ret_s.at[s], ret_r.at[s], along_blk(-(s + 1)))
        )

    for copy in copies3:
        copy.wait_recv()
    total = zx[0].astype(F32)
    for k in range(1, n_z):
        total += zx[k].astype(F32)
    total = total.astype(BF16)
    g2[0, y] = total[0:3]
    g2[1, x] = total[3:6]
    copies = []
    for k in (2, 1, 3):
        copies.append(send(g2.at[0, y], g2.at[0, y], ag2_s.at[0, k - 1], ag2_r.at[0, k - 1], along_y(k)))
        copies.append(send(g2.at[1, x], g2.at[1, x], ag2_s.at[1, k - 1], ag2_r.at[1, k - 1], along_x(k)))
    sends = list(copies)
    for copy in copies:
        copy.wait_recv()
    for h, at in ((0, x), (1, y)):
        for k in range(3):
            g1[h, at, 3 * k : 3 * k + 3] = g2[h, k]
        g1[h, at, 9] = g2[h, 3, 0]
    copies = []
    for k in (2, 1, 3):
        copies.append(send(g1.at[0, x], g1.at[0, x], ag1_s.at[0, k - 1], ag1_r.at[0, k - 1], along_x(k)))
        copies.append(send(g1.at[1, y], g1.at[1, y], ag1_s.at[1, k - 1], ag1_r.at[1, k - 1], along_y(k)))
    sends += copies
    handed = [
        send(g1.at[h, at], g_other.at[h, at], ag0_s.at[h, 0], ag0_r.at[h, 0], sibling)
        for h, at in ((0, x), (1, y))
    ]

    sy_copy.wait_recv()
    for copy in ret_copies:
        copy.wait_recv()
    total = (ssum[xh, core] + ssum_in[xh]) + half_in[...].astype(F32)
    total = total + (ret_in[0].astype(F32) + ret_in[1].astype(F32))
    ent_out[...] = total

    for i, k in ((1, 1), (2, 3), (0, 2)):
        copies[2 * i].wait_recv()
        copies[2 * i + 1].wait_recv()
        for h, at in ((0, x_at(4 - k)), (1, y_at(4 - k))):
            handed.append(
                send(g1.at[h, at], g_other.at[h, at], ag0_s.at[h, k], ag0_r.at[h, k], sibling)
            )

    def write(k, tiles):
        n = width // 16
        for t in range(3):
            rel_out[k, :, 128 * t : 128 * t + 128] = tiles[n * t : n * t + n].reshape(width, 128)
        rest = jnp.concatenate([tiles[3 * n + t].astype(F32) for t in range(4)], axis=1)
        rest = jnp.concatenate([rest, jnp.zeros((112, PAD), F32)], axis=0)
        rel_out[k, :, 384:width] = rest.T[:width, : width - 384].astype(BF16)

    write(core, g1[...].reshape(TILES, 16, 128))
    for copy in handed:
        copy.wait_recv()
    write(1 - core, g_other[...].reshape(TILES, 16, 128))

    for copy in slab_copies + forwards + [copy0, sy_copy] + handed + sends:
        copy.wait_send()
    for copy in tx_copies + copies1 + copies2 + copies3 + sx_copies + ret_copies:
        copy.wait_send()


def on_device(n_y, n_z, embeddings, relations, *lists):
    rows, width = embeddings.shape
    quarter = rows // 4
    span = lists[0].shape[1] // 2
    negs = lists[2].shape[2]
    dma = pltpu.SemaphoreType.DMA
    vmem, smem = pl.BlockSpec(memory_space=pltpu.VMEM), pl.BlockSpec(memory_space=pltpu.SMEM)

    def buffer(*shape, kind=F32):
        return pltpu.VMEM(shape, kind)

    scratch = [
        buffer(2, width, width, kind=BF16),
        buffer(2, 8, 1024, kind=I32),
        buffer(4, 8, 1024, kind=I32),
        buffer(4, 8, 1024, kind=I32),
        buffer(4, rows, PAD, kind=BF16),
        buffer(4, width, PAD, kind=BF16),
        buffer(4, width, PAD, kind=BF16),
        buffer(4, rows // 2, 128),
        buffer(2, 2, width, quarter, kind=BF16),
        buffer(rows // 2, width, kind=BF16),
        buffer(4, rows // 2, PAD, kind=BF16),
        buffer(4, rows // 2, PAD, kind=BF16),
        buffer(4, 8, PAD),
        buffer(4, width, 2 * PAD, kind=BF16),
        buffer(4, width, PAD, kind=BF16),
        buffer(2, TILES, 16, 128),
        buffer(TILES, 16, 128),
        buffer(TILES, 16, 128),
        buffer(2, 4, 10, 16, 128),
        buffer(2, 12, 16, 128),
        buffer(2, 4, 3, 16, 128),
        buffer(n_z, 6, 16, 128, kind=BF16),
        buffer(2, 4, 3, 16, 128, kind=BF16),
        buffer(2, 4, 10, 16, 128, kind=BF16),
        buffer(2, 4, 10, 16, 128, kind=BF16),
        buffer(2, 2, width, quarter),
        buffer(2, width, quarter),
        buffer(2, width, quarter, kind=BF16),
        buffer(2, width, quarter, kind=BF16),
        buffer(2, 2, width, quarter),
        buffer(2, width, quarter),
        buffer(width, quarter, kind=BF16),
        buffer(width, quarter, kind=BF16),
    ]
    for shape in (
        (3,), (2,), (2,), None, (2, 3), (2, 3), (n_z - 1,),
        (2, 3), (2, 3), (2, 4), (2,), (2,), (2,), None,
    ):
        scratch += [dma if shape is None else dma(shape)] * 2
    entity, relation = pl.pallas_call(
        functools.partial(kernel, n_y, n_z, span, negs),
        out_shape=(
            jax.ShapeDtypeStruct((width, quarter), F32),
            jax.ShapeDtypeStruct(relations.shape, BF16),
        ),
        in_specs=[vmem] * 5 + [smem] * 2,
        out_specs=(vmem, vmem),
        scratch_shapes=scratch,
        compiler_params=pltpu.CompilerParams(
            collective_id=0, has_side_effects=True, vmem_limit_bytes=56 * 2**20
        ),
    )(embeddings.T, relations, *lists[:-1], lists[-1].T)
    return entity.T, relation.astype(F32)


def solution(mesh):
    n_y = 4
    n_z = mesh.shape["blk"] // (2 * n_y)
    return jax.shard_map(
        functools.partial(on_device, n_y, n_z),
        mesh=mesh,
        in_specs=(
            P("blk", None),
            P(),
            P(None, ("blk", "rep")),
            P(None, ("blk", "rep")),
            P(None, ("blk", "rep"), None),
            P(None, ("blk", "rep")),
            P(None, ("blk", "rep")),
        ),
        out_specs=(P(("blk", "rep"), None), P()),
        check_vma=False,
    )
```

time: 86.5 us -> 70.7 us (0.82)
  the two profiles are of different devices: /device:TPU:1 before, /device:TPU:3 now
where the time goes in v2:
time: 70.7 us; the launch traced here: 70.6 us
  Pallas kernels  66.6 us (94%)
  other arithmetic  2.58 us (4%)
  local copies, waits for them, and re-layouts  0.76 us (1%)
    pallas_call x1, Pallas kernels, on_device(): pl.pallas_call(functools.partial(kernel, n_y, n_z, span, negs), out_shape...  66.6 us
    convert_element_type x1, other arithmetic, on_device(): return (entity.T, relation.astype(F32))  2.58 us

profile of v2, /device:TPU:3, one launch (start us, length us, event | category | flops | bytes accessed | tf_op | source)
XLA Modules:
  0.0 70.6 jit_solution(12996910292708225786)
XLA Ops:
  0.6 66.6 %shard_map.86 = (f32[400,256]{1,0:T(8,128)}, bf16[2,400,400]{2,1,0:T(8,128)(2,1)}) custom-call(bf16[400,1024]{1,0:T(8,128)(2,1)} %bitcast.3, bf16[2,400,400]{2,1,0:T(8,128)(2,1)} %rel.1, s32[2,1000]{1,0:T(2,128)} %src.1, s32[2,1000]{1,0:T(2,128)} %tgt.1, s32[2,2,1000]{2,1,0:T(2,128)} %neg.1, s32[2,2]{1,0:T(2,128)} %srel.1, s32[1,2]{1,0:T(1,128)} %bitcast.5), custom_call_target="tpu_custom_call" | custom-call | tf_op jit(solution)/shard_map/pallas_call | solution.py:429
  67.3 0.0 copy-start
  67.3 2.6 %convert_element_type.3 = f32[2,400,400]{2,1,0:T(8,128)} convert(bf16[2,400,400]{2,1,0:T(8,128)(2,1)} %get-tuple-element.5) | non-fusion elementwise | flops 320000 | bytes 1920000 | tf_op jit(solution)/shard_map/convert_element_type | solution.py:442
  69.9 0.0 copy-done
  69.9 0.8 %copy.10 = f32[256,400]{0,1:T(8,128)} copy(f32[256,400]{0,1:T(8,128)S(1)} %bitcast.4) | data formatting | bytes 819200
Async XLA Ops:
  67.3 2.6 %copy-start = (f32[400,256]{1,0:T(8,128)S(1)}, f32[400,256]{1,0:T(8,128)}, u32[]{:S(2)}) copy-start(f32[400,256]{1,0:T(8,128)} %get-tuple-element.4) | copy-start | bytes 1228804

commit v3 on v2

--- a/solution.py
+++ b/solution.py
@@ -34,12 +34,12 @@
 
 def kernel(
     n_y, n_z, span, negs,
-    emb, rel, src, tgt, neg, srel, ecnt,
+    emb_hbm, rel_hbm, src, tgt, neg, srel, ecnt,
     ent_out, rel_out,
-    opt, raw, lists, sel, ohs, svt, qt, cnt, slabt, slab, oht, ngm, pgs, qhl, sgt,
-    acc, acc_in, red, r1, s1, r2, zx, g2, g1, g_other,
+    emb, rel, opt, raw, lists, sel, ohs, svt, qt, cnt, slabt, slab, oht, ngm, pgs, qhl, sgt,
+    acc, acc_last, acc_in, red, red_out, r1, s1, r2, zx, g2, g1, g_other,
     tsum, tsum_in, ret, ret_in, ssum, ssum_in, half, half_in,
-    idx_s, idx_r, slab_s, slab_r, fwd_s, fwd_r, ar0_s, ar0_r, ar1_s, ar1_r, ar2_s, ar2_r, ar3_s, ar3_r,
+    load, idx_s, idx_r, slab_s, slab_r, fwd_s, fwd_r, ar0_s, ar0_r, ar1_s, ar1_r, ar2_s, ar2_r, ar3_s, ar3_r,
     ag2_s, ag2_r, ag1_s, ag1_r, ag0_s, ag0_r, tx_s, tx_r, ret_s, ret_r, sx_s, sx_r, sy_s, sy_r,
 ):
     width = emb.shape[0]
@@ -92,6 +92,12 @@
     for peer in peers:
         pl.semaphore_signal(barrier, inc=1, device_id=peer, device_id_type=MESH)
 
+    loads = [
+        pltpu.make_async_copy(emb_hbm, emb, load.at[0]),
+        pltpu.make_async_copy(rel_hbm, rel, load.at[1]),
+    ]
+    for copy in loads:
+        copy.start()
     lane = lax.broadcasted_iota(I32, (8, 1024), 1)
     row = lax.broadcasted_iota(I32, (8, 1024), 0)
     raw[...] = jnp.zeros(raw.shape, I32)
@@ -118,13 +124,16 @@
 
     index_copies = [
         send(lists.at[r], lists.at[r], idx_s.at[k - 1], idx_r.at[k - 1], along_rep(k))
-        for k in (1, 2, 3)
-    ]
+        for k in (2, 1, 3)
+    ]
+    here = pl.ds(pl.multiple_of(r * quarter, quarter), quarter)
     slab_copies = [
-        send(emb.at[:, pl.ds(pl.multiple_of(r * quarter, quarter), quarter)], slabt.at[s, core], slab_s.at[s], slab_r.at[s], along_blk(s + 1))
+        send(emb_hbm.at[:, here], slabt.at[s, core], slab_s.at[s], slab_r.at[s], along_blk(s + 1))
         for s in range(2)
     ]
 
+    for copy in loads:
+        copy.wait()
     unit = eye(width)
     for k in range(2):
         opt[k] = dot_nt(unit, rel[k]).astype(BF16)
@@ -188,7 +197,7 @@
         for h in range(2):
             slab[h * quarter : (h + 1) * quarter] = dot_nt(turn, slabt[s, h]).astype(BF16)
         turned = jnp.concatenate([slabt[s, 0], slabt[s, 1]], axis=1)
-        mains, rests, seconds = [], [], []
+        mains, seconds = [], []
         for j in range(2):
             at = 2 * s + j
             oht[at] = onehot(2 * quarter, 2 * xh * quarter, sel[at, 1:2, 0:PAD])
@@ -197,56 +206,64 @@
             positive = jnp.sum(query.astype(F32) * target, axis=0, keepdims=True)
             positive_grad = -sel[at, 4:5, 0:PAD].astype(F32) * jax.nn.sigmoid(-positive)
             pgs[at, 0:1] = positive_grad
-            for i in range(0, 2 * quarter, 128):
-                bent = jnp.tanh(dot(slab[i : i + 128], query))
-                times = jnp.concatenate([cnt[at, i : i + 128]] * (PAD // 128), axis=1)
-                ngm[at, i : i + 128] = (times * bent + times).astype(BF16)
+            bent = jnp.tanh(dot(slab[...], query))
+            times = jnp.concatenate([cnt[at]] * (PAD // 128), axis=1)
+            ngm[at] = (times * bent + times).astype(BF16)
             grad = positive_grad * target + dot(turned, ngm[at])
             high = grad.astype(BF16)
             qhl[at, :, 0:PAD] = high
             qhl[at, :, PAD:] = (grad - high.astype(F32)).astype(BF16)
             vectors = jnp.concatenate([svt[at]] * 2, axis=1)
-            mains.append(dot_nt(vectors, qhl[at, 0:384]))
-            rest = dot_nt(qhl[at, 384:width], vectors)
-            rests.append(jnp.concatenate([rest, jnp.zeros((16, PAD - width), F32)], axis=1))
+            mains.append(dot_nt(vectors, qhl[at]))
             seconds.append(sel[at, 3:4, 0:128].astype(F32))
-        n = width // 16
-        for k in range(2):
-            shares = [second if k else 1.0 - second for second in seconds]
-            for t in range(3):
-                tiles = sum(
-                    main[:, 128 * t : 128 * t + 128] * share for main, share in zip(mains, shares)
-                ).reshape(n, 16, 128)
-                acc[k, n * t : n * t + n] = tiles if s == 0 else acc[k, n * t : n * t + n] + tiles
-            for t in range(4):
-                tile = sum(
-                    rest[:, 128 * t : 128 * t + 128] * share for rest, share in zip(rests, shares)
-                )
-                acc[k, 3 * n + t] = tile if s == 0 else acc[k, 3 * n + t] + tile
-            if s == 0:
-                acc[k, 3 * n + 4] = jnp.zeros((16, 128), F32)
+        return mains, seconds
+
+    n = width // 16
+
+    def accumulate(s, k, mains, seconds):
+        first = jnp.where(k == 0, 1.0, 0.0)
+        shares = [first + second * (1.0 - 2.0 * first) for second in seconds]
+        for t in range(3):
+            tiles = sum(
+                main[:, 128 * t : 128 * t + 128] * share for main, share in zip(mains, shares)
+            ).reshape(n, 16, 128)
+            acc[k, n * t : n * t + n] = tiles if s == 0 else acc[k, n * t : n * t + n] + tiles
+        last = sum(
+            main[:, 384:width] * share[:, : width - 384] for main, share in zip(mains, shares)
+        )
+        last = jnp.concatenate([last, jnp.zeros((width, PAD - width), F32)], axis=1)
+        if s == 0:
+            acc_last[k] = last
+            return
+        last = acc_last[k] + last
+        last = jnp.concatenate([last, jnp.zeros((PAD - width, 128), F32)], axis=0).T
+        for t in range(4):
+            acc[k, 3 * n + t] = last[:16, 128 * t : 128 * t + 128]
+        acc[k, 3 * n + 4] = jnp.zeros((16, 128), F32)
 
     queries(0)
     queries(1)
     forwards = [forward(0)]
     forwards[0].wait_recv()
-    score(0)
+    found = score(0)
+    for k in range(2):
+        accumulate(0, k, *found)
     forwards.append(forward(1))
     forwards[1].wait_recv()
-    score(1)
-
+    found = score(1)
+    accumulate(1, 1 - core, *found)
     copy0 = send(acc.at[1 - core], acc_in, ar0_s, ar0_r, sibling)
+    accumulate(1, core, *found)
     copy0.wait_recv()
     red[...] = acc[core] + acc_in[...]
-    r1[0, x] = red[pl.ds(10 * x, 10)]
-    r1[1, y] = red[pl.ds(40 + 10 * y, 10)]
+    red_out[...] = red[...].astype(BF16)
     copies1 = []
     for k in (2, 1, 3):
         copies1.append(
-            send(red.at[pl.ds(10 * x_at(k), 10)], r1.at[0, x], ar1_s.at[0, k - 1], ar1_r.at[0, k - 1], along_x(k))
+            send(red_out.at[pl.ds(10 * x_at(k), 10)], r1.at[0, k - 1], ar1_s.at[0, k - 1], ar1_r.at[0, k - 1], along_x(k))
         )
         copies1.append(
-            send(red.at[pl.ds(40 + 10 * y_at(k), 10)], r1.at[1, y], ar1_s.at[1, k - 1], ar1_r.at[1, k - 1], along_y(k))
+            send(red_out.at[pl.ds(40 + 10 * y_at(k), 10)], r1.at[1, k - 1], ar1_s.at[1, k - 1], ar1_r.at[1, k - 1], along_y(k))
         )
 
     for s in range(2):
@@ -277,8 +294,11 @@
 
     for copy in copies1:
         copy.wait_recv()
-    for h in range(2):
-        s1[h, 0:10] = (r1[h, 0] + r1[h, 1]) + (r1[h, 2] + r1[h, 3])
+    for h, at in ((0, 10 * x), (1, 40 + 10 * y)):
+        total = red[pl.ds(at, 10)]
+        for k in range(3):
+            total += r1[h, k].astype(F32)
+        s1[h, 0:10] = total
     r2[0, y] = s1[0, pl.ds(3 * y, 3)]
     r2[1, x] = s1[1, pl.ds(3 * x, 3)]
     copies2 = []
@@ -357,7 +377,6 @@
             )
 
     def write(k, tiles):
-        n = width // 16
         for t in range(3):
             rel_out[k, :, 128 * t : 128 * t + 128] = tiles[n * t : n * t + n].reshape(width, 128)
         rest = jnp.concatenate([tiles[3 * n + t].astype(F32) for t in range(4)], axis=1)
@@ -373,6 +392,11 @@
         copy.wait_send()
     for copy in tx_copies + copies1 + copies2 + copies3 + sx_copies + ret_copies:
         copy.wait_send()
+
+
+def hand_over(entity, relation, entity_out, relation_out):
+    entity_out[...] = entity[...]
+    relation_out[...] = relation[...].astype(F32)
 
 
 def on_device(n_y, n_z, embeddings, relations, *lists):
@@ -387,6 +411,8 @@
         return pltpu.VMEM(shape, kind)
 
     scratch = [
+        buffer(*embeddings.shape[::-1], kind=BF16),
+        buffer(2, width, width, kind=BF16),
         buffer(2, width, width, kind=BF16),
         buffer(2, 8, 1024, kind=I32),
         buffer(4, 8, 1024, kind=I32),
@@ -403,9 +429,11 @@
         buffer(4, width, 2 * PAD, kind=BF16),
         buffer(4, width, PAD, kind=BF16),
         buffer(2, TILES, 16, 128),
+        buffer(2, width, 128),
         buffer(TILES, 16, 128),
         buffer(TILES, 16, 128),
-        buffer(2, 4, 10, 16, 128),
+        buffer(TILES, 16, 128, kind=BF16),
+        buffer(2, 3, 10, 16, 128, kind=BF16),
         buffer(2, 12, 16, 128),
         buffer(2, 4, 3, 16, 128),
         buffer(n_z, 6, 16, 128, kind=BF16),
@@ -420,6 +448,7 @@
         buffer(2, width, quarter),
         buffer(width, quarter, kind=BF16),
         buffer(width, quarter, kind=BF16),
+        dma((2,)),
     ]
     for shape in (
         (3,), (2,), (2,), None, (2, 3), (2, 3), (n_z - 1,),
@@ -432,14 +461,23 @@
             jax.ShapeDtypeStruct((width, quarter), F32),
             jax.ShapeDtypeStruct(relations.shape, BF16),
         ),
-        in_specs=[vmem] * 5 + [smem] * 2,
+        in_specs=[pl.BlockSpec(memory_space=pl.ANY)] * 2 + [vmem] * 3 + [smem] * 2,
         out_specs=(vmem, vmem),
         scratch_shapes=scratch,
         compiler_params=pltpu.CompilerParams(
             collective_id=0, has_side_effects=True, vmem_limit_bytes=56 * 2**20
         ),
     )(embeddings.T, relations, *lists[:-1], lists[-1].T)
-    return entity.T, relation.astype(F32)
+    entity, relation = pl.pallas_call(
+        hand_over,
+        out_shape=(
+            jax.ShapeDtypeStruct(entity.shape, F32),
+            jax.ShapeDtypeStruct(relation.shape, F32),
+        ),
+        in_specs=[vmem] * 2,
+        out_specs=(vmem, vmem),
+    )(entity, relation)
+    return entity.T, relation
 
 
 def solution(mesh):

time: 70.7 us -> 68.7 us (0.972)
  other arithmetic: 2.58 us -> 0 us
  Pallas kernels: 66.6 us -> 67.9 us
  local copies, waits for them, and re-layouts: 0.76 us -> 0 us
    pallas_call x0 -> x1, Pallas kernels: none -> 2.6 us  [on_device(): pl.pallas_call(hand_over, out_shape=(jax.ShapeDtypeStruct(entity.shape, F...]
    convert_element_type x1 -> x0, other arithmetic: 2.58 us -> none  [on_device(): return (entity.T, relation.astype(F32))]
    pallas_call x1, Pallas kernels: 66.6 us -> 65.3 us  [on_device(): pl.pallas_call(functools.partial(kernel, n_y, n_z, span, negs), out_shape...]
    unnamed x3 -> x0, local copies, waits for them, and re-layouts: 0.76 us -> none
where the time goes in v3:
time: 68.7 us; the launch traced here: 68.5 us
  Pallas kernels  67.9 us (99%)
    pallas_call x1, Pallas kernels, on_device(): pl.pallas_call(functools.partial(kernel, n_y, n_z, span, negs), out_shape...  65.3 us
    pallas_call x1, Pallas kernels, on_device(): pl.pallas_call(hand_over, out_shape=(jax.ShapeDtypeStruct(entity.shape, F...  2.6 us

profile of v3, /device:TPU:3, one launch (start us, length us, event | category | flops | bytes accessed | tf_op | source)
XLA Modules:
  0.0 68.5 jit_solution(1366112879700484213)
XLA Ops:
  0.6 65.3 %shard_map.86 = (f32[400,256]{1,0:T(8,128)}, bf16[2,400,400]{2,1,0:T(8,128)(2,1)}) custom-call(bf16[400,1024]{1,0:T(8,128)(2,1)} %bitcast.3, bf16[2,400,400]{2,1,0:T(8,128)(2,1)} %rel_hbm.1, s32[2,1000]{1,0:T(2,128)} %src.1, s32[2,1000]{1,0:T(2,128)} %tgt.1, s32[2,2,1000]{2,1,0:T(2,128)} %neg.1, s32[2,2]{1,0:T(2,128)} %srel.1, s32[1,2]{1,0:T(1,128)} %bitcast.4), custom_call_target="tpu_custom_call" | custom-call | tf_op jit(solution)/shard_map/pallas_call | solution.py:458
  65.9 2.6 %shard_map.87 = (f32[400,256]{1,0:T(8,128)}, f32[2,400,400]{2,1,0:T(8,128)}) custom-call(f32[400,256]{1,0:T(8,128)} %get-tuple-element.6.entity, bf16[2,400,400]{2,1,0:T(8,128)(2,1)} %get-tuple-element.7.relation), custom_call_target="tpu_custom_call" | custom-call | tf_op jit(solution)/shard_map/pallas_call | solution.py:471

commit v4 on v3

--- a/solution.py
+++ b/solution.py
@@ -51,6 +51,7 @@
     x = xh * 2 + xl
     sibling = (b, xh * 2 + 1 - core)
     mate = (b, (1 - xh) * 2 + core)
+    partner = (b + 1 - 2 * xl, r)
 
     def along_blk(k):
         return (lax.rem(b + k + n_blk, n_blk), r)
@@ -127,10 +128,13 @@
         for k in (2, 1, 3)
     ]
     here = pl.ds(pl.multiple_of(r * quarter, quarter), quarter)
-    slab_copies = [
-        send(emb_hbm.at[:, here], slabt.at[s, core], slab_s.at[s], slab_r.at[s], along_blk(s + 1))
-        for s in range(2)
-    ]
+
+    def send_slab(s):
+        return send(
+            emb_hbm.at[:, here], slabt.at[s, core], slab_s.at[s], slab_r.at[s], along_blk(s + 1)
+        )
+
+    slab_copies = {1: send_slab(1)}
 
     for copy in loads:
         copy.wait()
@@ -170,6 +174,9 @@
             sel[at, 3:4, :] = meta_words[j] & 1
             sel[at, 4:5, 0:PAD] = valid.astype(I32)
 
+    slab_copies[1].wait_send()
+    slab_copies[0] = send_slab(0)
+
     def operator(table, at):
         second = sel[at, 3:4, 0:width].astype(F32)
         return (
@@ -192,13 +199,15 @@
             slabt.at[s, core], slabt.at[s, core], fwd_s.at[s], fwd_r.at[s], sibling
         )
 
-    def score(s):
+    def halve(s):
         turn = eye(quarter) * jnp.asarray(0.5, BF16)
         for h in range(2):
             slab[h * quarter : (h + 1) * quarter] = dot_nt(turn, slabt[s, h]).astype(BF16)
+
+    def score(s, js):
         turned = jnp.concatenate([slabt[s, 0], slabt[s, 1]], axis=1)
         mains, seconds = [], []
-        for j in range(2):
+        for j in js:
             at = 2 * s + j
             oht[at] = onehot(2 * quarter, 2 * xh * quarter, sel[at, 1:2, 0:PAD])
             query = qt[at]
@@ -227,12 +236,12 @@
             tiles = sum(
                 main[:, 128 * t : 128 * t + 128] * share for main, share in zip(mains, shares)
             ).reshape(n, 16, 128)
-            acc[k, n * t : n * t + n] = tiles if s == 0 else acc[k, n * t : n * t + n] + tiles
+            acc[k, n * t : n * t + n] = tiles if s == 1 else acc[k, n * t : n * t + n] + tiles
         last = sum(
             main[:, 384:width] * share[:, : width - 384] for main, share in zip(mains, shares)
         )
         last = jnp.concatenate([last, jnp.zeros((width, PAD - width), F32)], axis=1)
-        if s == 0:
+        if s == 1:
             acc_last[k] = last
             return
         last = acc_last[k] + last
@@ -241,19 +250,22 @@
             acc[k, 3 * n + t] = last[:16, 128 * t : 128 * t + 128]
         acc[k, 3 * n + 4] = jnp.zeros((16, 128), F32)
 
+    queries(1)
+    forwards = [forward(1)]
     queries(0)
-    queries(1)
-    forwards = [forward(0)]
     forwards[0].wait_recv()
-    found = score(0)
+    halve(1)
+    one = score(1, (0,))
+    forwards.append(forward(0))
+    two = score(1, (1,))
     for k in range(2):
-        accumulate(0, k, *found)
-    forwards.append(forward(1))
+        accumulate(1, k, one[0] + two[0], one[1] + two[1])
     forwards[1].wait_recv()
-    found = score(1)
-    accumulate(1, 1 - core, *found)
+    halve(0)
+    found = score(0, (0, 1))
+    accumulate(0, 1 - core, *found)
     copy0 = send(acc.at[1 - core], acc_in, ar0_s, ar0_r, sibling)
-    accumulate(1, core, *found)
+    accumulate(0, core, *found)
     copy0.wait_recv()
     red[...] = acc[core] + acc_in[...]
     red_out[...] = red[...].astype(BF16)
@@ -283,14 +295,10 @@
         both = jnp.concatenate([qhl[at, :, 0:PAD], qhl[at, :, PAD:]], axis=0)
         sgt[at] = dot(jnp.concatenate([turned, turned], axis=1), both).astype(BF16)
 
-    left = jnp.concatenate([sgt[at] for at in range(4)], axis=1)
-    for q in range(4):
-        rows = slice(q * quarter, (q + 1) * quarter)
-        ssum[q // 2, q % 2] = dot_nt(left, jnp.concatenate([ohs[at, rows] for at in range(4)], axis=1))
-    sx_copies = [
-        send(ssum.at[h, 1 - core], ssum_in.at[h], sx_s.at[h], sx_r.at[h], sibling)
-        for h in range(2)
-    ]
+    for copy in tx_copies:
+        copy.wait_recv()
+    ret[0] = (tsum[0, core] + tsum_in[0]).astype(BF16)
+    ret_copies = [send(ret.at[0], ret_in.at[0], ret_s.at[0], ret_r.at[0], partner)]
 
     for copy in copies1:
         copy.wait_recv()
@@ -310,6 +318,15 @@
             send(s1.at[1, pl.ds(3 * x_at(k), 3)], r2.at[1, x], ar2_s.at[1, k - 1], ar2_r.at[1, k - 1], along_x(k))
         )
 
+    left = jnp.concatenate([sgt[at] for at in range(4)], axis=1)
+    for q in range(4):
+        rows = slice(q * quarter, (q + 1) * quarter)
+        ssum[q // 2, q % 2] = dot_nt(left, jnp.concatenate([ohs[at, rows] for at in range(4)], axis=1))
+    sx_copies = [
+        send(ssum.at[h, 1 - core], ssum_in.at[h], sx_s.at[h], sx_r.at[h], sibling)
+        for h in range(2)
+    ]
+
     for copy in copies2:
         copy.wait_recv()
     for h in range(2):
@@ -320,18 +337,14 @@
         for k in sorted(range(1, n_z), key=lambda k: -min(k, n_z - k))
     ]
 
+    ret_copies[0].wait_recv()
+    passed = ret_in[0].astype(F32) * jnp.where(xl == 1, 1.0, 0.0)
+    ret[1] = (tsum[1, core] + tsum_in[1] + passed).astype(BF16)
+    ret_copies.append(send(ret.at[1], ret_in.at[1], ret_s.at[1], ret_r.at[1], along_blk(-2)))
     for copy in sx_copies:
         copy.wait_recv()
     half[...] = (ssum[1 - xh, core] + ssum_in[1 - xh]).astype(BF16)
     sy_copy = send(half, half_in, sy_s, sy_r, mate)
-    ret_copies = []
-    for s in range(2):
-        tx_copies[s].wait_recv()
-        ret[s] = (tsum[s, core] + tsum_in[s]).astype(BF16)
-        ret_copies.append(
-            send(ret.at[s], ret_in.at[s], ret_s.at[s], ret_r.at[s], along_blk(-(s + 1)))
-        )
-
     for copy in copies3:
         copy.wait_recv()
     total = zx[0].astype(F32)
@@ -362,10 +375,10 @@
     ]
 
     sy_copy.wait_recv()
-    for copy in ret_copies:
-        copy.wait_recv()
+    ret_copies[1].wait_recv()
     total = (ssum[xh, core] + ssum_in[xh]) + half_in[...].astype(F32)
-    total = total + (ret_in[0].astype(F32) + ret_in[1].astype(F32))
+    mine = ret_in[0].astype(F32) * jnp.where(xl == 0, 1.0, 0.0)
+    total = total + (mine + ret_in[1].astype(F32))
     ent_out[...] = total
 
     for i, k in ((1, 1), (2, 3), (0, 2)):
@@ -388,7 +401,7 @@
         copy.wait_recv()
     write(1 - core, g_other[...].reshape(TILES, 16, 128))
 
-    for copy in slab_copies + forwards + [copy0, sy_copy] + handed + sends:
+    for copy in [slab_copies[0]] + forwards + [copy0, sy_copy] + handed + sends:
         copy.wait_send()
     for copy in tx_copies + copies1 + copies2 + copies3 + sx_copies + ret_copies:
         copy.wait_send()

time: 68.7 us -> 65.6 us (0.955)
  the two profiles are of different devices: /device:TPU:3 before, /device:TPU:1 now
where the time goes in v4:
time: 65.6 us; the launch traced here: 65.4 us
  Pallas kernels  64.8 us (99%)
    pallas_call x1, Pallas kernels, on_device(): pl.pallas_call(functools.partial(kernel, n_y, n_z, span, negs), out_shape...  62.2 us
    pallas_call x1, Pallas kernels, on_device(): pl.pallas_call(hand_over, out_shape=(jax.ShapeDtypeStruct(entity.shape, F...  2.6 us

profile of v4, /device:TPU:1, one launch (start us, length us, event | category | flops | bytes accessed | tf_op | source)
XLA Modules:
  0.0 65.4 jit_solution(13610554169334532442)
XLA Ops:
  0.6 62.2 %shard_map.86 = (f32[400,256]{1,0:T(8,128)}, bf16[2,400,400]{2,1,0:T(8,128)(2,1)}) custom-call(bf16[400,1024]{1,0:T(8,128)(2,1)} %bitcast.3, bf16[2,400,400]{2,1,0:T(8,128)(2,1)} %rel_hbm.1, s32[2,1000]{1,0:T(2,128)} %src.1, s32[2,1000]{1,0:T(2,128)} %tgt.1, s32[2,2,1000]{2,1,0:T(2,128)} %neg.1, s32[2,2]{1,0:T(2,128)} %srel.1, s32[1,2]{1,0:T(1,128)} %bitcast.4), custom_call_target="tpu_custom_call" | custom-call | tf_op jit(solution)/shard_map/pallas_call | solution.py:471
  62.8 2.6 %shard_map.87 = (f32[400,256]{1,0:T(8,128)}, f32[2,400,400]{2,1,0:T(8,128)}) custom-call(f32[400,256]{1,0:T(8,128)} %get-tuple-element.6.entity, bf16[2,400,400]{2,1,0:T(8,128)(2,1)} %get-tuple-element.7.relation), custom_call_target="tpu_custom_call" | custom-call | tf_op jit(solution)/shard_map/pallas_call | solution.py:484

commit v5 on v4

--- a/solution.py
+++ b/solution.py
@@ -222,8 +222,7 @@
             high = grad.astype(BF16)
             qhl[at, :, 0:PAD] = high
             qhl[at, :, PAD:] = (grad - high.astype(F32)).astype(BF16)
-            vectors = jnp.concatenate([svt[at]] * 2, axis=1)
-            mains.append(dot_nt(vectors, qhl[at]))
+            mains.append(dot_nt(svt[at], high))
             seconds.append(sel[at, 3:4, 0:128].astype(F32))
         return mains, seconds
 
@@ -295,11 +294,6 @@
         both = jnp.concatenate([qhl[at, :, 0:PAD], qhl[at, :, PAD:]], axis=0)
         sgt[at] = dot(jnp.concatenate([turned, turned], axis=1), both).astype(BF16)
 
-    for copy in tx_copies:
-        copy.wait_recv()
-    ret[0] = (tsum[0, core] + tsum_in[0]).astype(BF16)
-    ret_copies = [send(ret.at[0], ret_in.at[0], ret_s.at[0], ret_r.at[0], partner)]
-
     for copy in copies1:
         copy.wait_recv()
     for h, at in ((0, 10 * x), (1, 40 + 10 * y)):
@@ -310,13 +304,18 @@
     r2[0, y] = s1[0, pl.ds(3 * y, 3)]
     r2[1, x] = s1[1, pl.ds(3 * x, 3)]
     copies2 = []
-    for k in range(1, 4):
+    for k in (2, 1, 3):
         copies2.append(
             send(s1.at[0, pl.ds(3 * y_at(k), 3)], r2.at[0, y], ar2_s.at[0, k - 1], ar2_r.at[0, k - 1], along_y(k))
         )
         copies2.append(
             send(s1.at[1, pl.ds(3 * x_at(k), 3)], r2.at[1, x], ar2_s.at[1, k - 1], ar2_r.at[1, k - 1], along_x(k))
         )
+
+    for copy in tx_copies:
+        copy.wait_recv()
+    ret[0] = (tsum[0, core] + tsum_in[0]).astype(BF16)
+    ret_copies = [send(ret.at[0], ret_in.at[0], ret_s.at[0], ret_r.at[0], partner)]
 
     left = jnp.concatenate([sgt[at] for at in range(4)], axis=1)
     for q in range(4):
@@ -337,14 +336,14 @@
         for k in sorted(range(1, n_z), key=lambda k: -min(k, n_z - k))
     ]
 
+    for copy in sx_copies:
+        copy.wait_recv()
+    half[...] = (ssum[1 - xh, core] + ssum_in[1 - xh]).astype(BF16)
+    sy_copy = send(half, half_in, sy_s, sy_r, mate)
     ret_copies[0].wait_recv()
     passed = ret_in[0].astype(F32) * jnp.where(xl == 1, 1.0, 0.0)
     ret[1] = (tsum[1, core] + tsum_in[1] + passed).astype(BF16)
     ret_copies.append(send(ret.at[1], ret_in.at[1], ret_s.at[1], ret_r.at[1], along_blk(-2)))
-    for copy in sx_copies:
-        copy.wait_recv()
-    half[...] = (ssum[1 - xh, core] + ssum_in[1 - xh]).astype(BF16)
-    sy_copy = send(half, half_in, sy_s, sy_r, mate)
     for copy in copies3:
         copy.wait_recv()
     total = zx[0].astype(F32)
@@ -481,14 +480,19 @@
             collective_id=0, has_side_effects=True, vmem_limit_bytes=56 * 2**20
         ),
     )(embeddings.T, relations, *lists[:-1], lists[-1].T)
+    blocks = [
+        pl.BlockSpec((width // 2, quarter), lambda i: (i, 0)),
+        pl.BlockSpec((1, width, width), lambda i: (i, 0, 0)),
+    ]
     entity, relation = pl.pallas_call(
         hand_over,
         out_shape=(
             jax.ShapeDtypeStruct(entity.shape, F32),
             jax.ShapeDtypeStruct(relation.shape, F32),
         ),
-        in_specs=[vmem] * 2,
-        out_specs=(vmem, vmem),
+        grid=(2,),
+        in_specs=blocks,
+        out_specs=tuple(blocks),
     )(entity, relation)
     return entity.T, relation
 

time: 65.6 us -> 60.2 us (0.918)
  Pallas kernels: 64.8 us -> 59.3 us
    pallas_call x1, Pallas kernels: 62.2 us -> 56.9 us  [on_device(): pl.pallas_call(functools.partial(kernel, n_y, n_z, span, negs), out_shape...]
where the time goes in v5:
time: 60.2 us; the launch traced here: 60 us
  Pallas kernels  59.3 us (99%)
  between operations  0.64 us (1%)
    pallas_call x1, Pallas kernels, on_device(): pl.pallas_call(functools.partial(kernel, n_y, n_z, span, negs), out_shape...  56.9 us
    pallas_call x1, Pallas kernels, on_device(): pl.pallas_call(hand_over, out_shape=(jax.ShapeDtypeStruct(entity.shape, F...  2.47 us

profile of v5, /device:TPU:1, one launch (start us, length us, event | category | flops | bytes accessed | tf_op | source)
XLA Modules:
  0.0 60.0 jit_solution(6048979291406582564)
XLA Ops:
  0.6 56.9 %shard_map.86 = (f32[400,256]{1,0:T(8,128)}, bf16[2,400,400]{2,1,0:T(8,128)(2,1)}) custom-call(bf16[400,1024]{1,0:T(8,128)(2,1)} %bitcast.3, bf16[2,400,400]{2,1,0:T(8,128)(2,1)} %rel_hbm.1, s32[2,1000]{1,0:T(2,128)} %src.1, s32[2,1000]{1,0:T(2,128)} %tgt.1, s32[2,2,1000]{2,1,0:T(2,128)} %neg.1, s32[2,2]{1,0:T(2,128)} %srel.1, s32[1,2]{1,0:T(1,128)} %bitcast.4), custom_call_target="tpu_custom_call" | custom-call | tf_op jit(solution)/shard_map/pallas_call | solution.py:470
  57.5 2.5 %shard_map.87 = (f32[400,256]{1,0:T(8,128)}, f32[2,400,400]{2,1,0:T(8,128)}) custom-call(f32[400,256]{1,0:T(8,128)} %get-tuple-element.6.entity, bf16[2,400,400]{2,1,0:T(8,128)(2,1)} %get-tuple-element.7.relation), custom_call_target="tpu_custom_call" | custom-call | tf_op jit(solution)/shard_map/pallas_call | solution.py:487

commit v6 on v5

--- a/solution.py
+++ b/solution.py
@@ -37,7 +37,7 @@
     emb_hbm, rel_hbm, src, tgt, neg, srel, ecnt,
     ent_out, rel_out,
     emb, rel, opt, raw, lists, sel, ohs, svt, qt, cnt, slabt, slab, oht, ngm, pgs, qhl, sgt,
-    acc, acc_last, acc_in, red, red_out, r1, s1, r2, zx, g2, g1, g_other,
+    acc, acc_last, acc_out, acc_in, red, red_out, r1, s1, r2, zx, g2, g1, g_other,
     tsum, tsum_in, ret, ret_in, ssum, ssum_in, half, half_in,
     load, idx_s, idx_r, slab_s, slab_r, fwd_s, fwd_r, ar0_s, ar0_r, ar1_s, ar1_r, ar2_s, ar2_r, ar3_s, ar3_r,
     ag2_s, ag2_r, ag1_s, ag1_r, ag0_s, ag0_r, tx_s, tx_r, ret_s, ret_r, sx_s, sx_r, sy_s, sy_r,
@@ -263,10 +263,11 @@
     halve(0)
     found = score(0, (0, 1))
     accumulate(0, 1 - core, *found)
-    copy0 = send(acc.at[1 - core], acc_in, ar0_s, ar0_r, sibling)
+    acc_out[...] = acc[1 - core].astype(BF16)
+    copy0 = send(acc_out, acc_in, ar0_s, ar0_r, sibling)
     accumulate(0, core, *found)
     copy0.wait_recv()
-    red[...] = acc[core] + acc_in[...]
+    red[...] = acc[core] + acc_in[...].astype(F32)
     red_out[...] = red[...].astype(BF16)
     copies1 = []
     for k in (2, 1, 3):
@@ -373,13 +374,6 @@
         for h, at in ((0, x), (1, y))
     ]
 
-    sy_copy.wait_recv()
-    ret_copies[1].wait_recv()
-    total = (ssum[xh, core] + ssum_in[xh]) + half_in[...].astype(F32)
-    mine = ret_in[0].astype(F32) * jnp.where(xl == 0, 1.0, 0.0)
-    total = total + (mine + ret_in[1].astype(F32))
-    ent_out[...] = total
-
     for i, k in ((1, 1), (2, 3), (0, 2)):
         copies[2 * i].wait_recv()
         copies[2 * i + 1].wait_recv()
@@ -394,6 +388,13 @@
         rest = jnp.concatenate([tiles[3 * n + t].astype(F32) for t in range(4)], axis=1)
         rest = jnp.concatenate([rest, jnp.zeros((112, PAD), F32)], axis=0)
         rel_out[k, :, 384:width] = rest.T[:width, : width - 384].astype(BF16)
+
+    sy_copy.wait_recv()
+    ret_copies[1].wait_recv()
+    total = (ssum[xh, core] + ssum_in[xh]) + half_in[...].astype(F32)
+    mine = ret_in[0].astype(F32) * jnp.where(xl == 0, 1.0, 0.0)
+    total = total + (mine + ret_in[1].astype(F32))
+    ent_out[...] = total
 
     write(core, g1[...].reshape(TILES, 16, 128))
     for copy in handed:
@@ -442,7 +443,8 @@
         buffer(4, width, PAD, kind=BF16),
         buffer(2, TILES, 16, 128),
         buffer(2, width, 128),
-        buffer(TILES, 16, 128),
+        buffer(TILES, 16, 128, kind=BF16),
+        buffer(TILES, 16, 128, kind=BF16),
         buffer(TILES, 16, 128),
         buffer(TILES, 16, 128, kind=BF16),
         buffer(2, 3, 10, 16, 128, kind=BF16),

time: 60.2 us -> 59.8 us (level)
  no operation moved by 1% of the time
where the time goes in v6:
time: 59.8 us; the launch traced here: 59.6 us
  Pallas kernels  58.9 us (98%)
  between operations  0.64 us (1%)
    pallas_call x1, Pallas kernels, on_device(): pl.pallas_call(functools.partial(kernel, n_y, n_z, span, negs), out_shape...  56.5 us
    pallas_call x1, Pallas kernels, on_device(): pl.pallas_call(hand_over, out_shape=(jax.ShapeDtypeStruct(entity.shape, F...  2.47 us

profile of v6, /device:TPU:1, one launch (start us, length us, event | category | flops | bytes accessed | tf_op | source)
XLA Modules:
  0.0 59.6 jit_solution(10902548919054401541)
XLA Ops:
  0.6 56.5 %shard_map.86 = (f32[400,256]{1,0:T(8,128)}, bf16[2,400,400]{2,1,0:T(8,128)(2,1)}) custom-call(bf16[400,1024]{1,0:T(8,128)(2,1)} %bitcast.3, bf16[2,400,400]{2,1,0:T(8,128)(2,1)} %rel_hbm.1, s32[2,1000]{1,0:T(2,128)} %src.1, s32[2,1000]{1,0:T(2,128)} %tgt.1, s32[2,2,1000]{2,1,0:T(2,128)} %neg.1, s32[2,2]{1,0:T(2,128)} %srel.1, s32[1,2]{1,0:T(1,128)} %bitcast.4), custom_call_target="tpu_custom_call" | custom-call | tf_op jit(solution)/shard_map/pallas_call | solution.py:472
  57.1 2.5 %shard_map.87 = (f32[400,256]{1,0:T(8,128)}, f32[2,400,400]{2,1,0:T(8,128)}) custom-call(f32[400,256]{1,0:T(8,128)} %get-tuple-element.6.entity, bf16[2,400,400]{2,1,0:T(8,128)(2,1)} %get-tuple-element.7.relation), custom_call_target="tpu_custom_call" | custom-call | tf_op jit(solution)/shard_map/pallas_call | solution.py:489

commit v7 on v6

--- a/solution.py
+++ b/solution.py
@@ -187,6 +187,7 @@
         for j in range(2):
             at = 2 * s + j
             ohs[at] = onehot(4 * quarter, 0, sel[at, 0:1, 0:PAD])
+            oht[at] = onehot(2 * quarter, 2 * xh * quarter, sel[at, 1:2, 0:PAD])
             vectors = dot(emb[...], ohs[at]).astype(BF16)
             svt[at] = vectors
             qt[at] = dot(operator(opt, at), vectors).astype(BF16)
@@ -209,7 +210,6 @@
         mains, seconds = [], []
         for j in js:
             at = 2 * s + j
-            oht[at] = onehot(2 * quarter, 2 * xh * quarter, sel[at, 1:2, 0:PAD])
             query = qt[at]
             target = dot(turned, oht[at])
             positive = jnp.sum(query.astype(F32) * target, axis=0, keepdims=True)

time: 59.8 us -> 60 us (level)
  no operation moved by 1% of the time
where the time goes in v7:
time: 60 us; the launch traced here: 59.9 us
  Pallas kernels  59.2 us (99%)
  between operations  0.64 us (1%)
    pallas_call x1, Pallas kernels, on_device(): pl.pallas_call(functools.partial(kernel, n_y, n_z, span, negs), out_shape...  56.7 us
    pallas_call x1, Pallas kernels, on_device(): pl.pallas_call(hand_over, out_shape=(jax.ShapeDtypeStruct(entity.shape, F...  2.47 us

profile of v7, /device:TPU:1, one launch (start us, length us, event | category | flops | bytes accessed | tf_op | source)
XLA Modules:
  0.0 59.9 jit_solution(14214037574151793190)
XLA Ops:
  0.6 56.7 %shard_map.86 = (f32[400,256]{1,0:T(8,128)}, bf16[2,400,400]{2,1,0:T(8,128)(2,1)}) custom-call(bf16[400,1024]{1,0:T(8,128)(2,1)} %bitcast.3, bf16[2,400,400]{2,1,0:T(8,128)(2,1)} %rel_hbm.1, s32[2,1000]{1,0:T(2,128)} %src.1, s32[2,1000]{1,0:T(2,128)} %tgt.1, s32[2,2,1000]{2,1,0:T(2,128)} %neg.1, s32[2,2]{1,0:T(2,128)} %srel.1, s32[1,2]{1,0:T(1,128)} %bitcast.4), custom_call_target="tpu_custom_call" | custom-call | tf_op jit(solution)/shard_map/pallas_call | solution.py:472
  57.4 2.5 %shard_map.87 = (f32[400,256]{1,0:T(8,128)}, f32[2,400,400]{2,1,0:T(8,128)}) custom-call(f32[400,256]{1,0:T(8,128)} %get-tuple-element.6.entity, bf16[2,400,400]{2,1,0:T(8,128)(2,1)} %get-tuple-element.7.relation), custom_call_target="tpu_custom_call" | custom-call | tf_op jit(solution)/shard_map/pallas_call | solution.py:489
